TPU v7x, 512 devices: a whole 4x8x8 slice. The times are simulated.
512 devices in a mesh: cuts: 4 (over x), dev: 128 (over z, y, core).
Axes of the slice: x: 4, y: 8, z: 8, core: 2. Of those that a mesh axis runs over, the one named last changes fastest.
Arguments:
- kv_cache: bfloat16 [4096, 128, 2048], P(('cuts', 'dev')), may hold values from -6 to 6
- queries: bfloat16 [4, 128, 768, 128], P('cuts', 'dev'), may hold values from -6 to 6
- gates: bfloat16 [4, 16, 768, 1024], P('cuts', None, 'dev'), may hold values from -6 to 6
- tokens: bfloat16 [4, 16, 768, 1024], P('cuts', None, 'dev'), may hold values from -6 to 6
- w_out: bfloat16 [1024, 1024], P('dev'), may hold values from -0.1875 to 0.1875
- norm_gain: float32 [1024], replicated, may hold values from 0.1 to 1.9
- hist_blocks: int32 [4, 64], replicated, may hold values from 1 to 32, as said below
- ranker_list: int32 [4, 64], replicated, may hold values from 0 to 63, as said below
- owner_ids: int32 [4, 64, 32], replicated, may hold values from -1 to 511, as said below
- slot_ids: int32 [4, 64, 32], replicated, may hold values from -1 to 7, as said below
- block_mask: int32 [4, 64, 6, 32], replicated, may hold values 0 or 1
Outputs:
- mixed: bfloat16 [4, 16, 768, 1024], P('cuts', None, 'dev')
Inputs may be any that keep to these rules, and one draw needn't show every extreme that they name: `hist_blocks`: the entries of one slice sum to 1024, and one request of each slice has exactly 32 blocks. `ranker_list`: each slice's row is a permutation of its 64 requests. `owner_ids`: an entry is the cut index times 128 plus the dev index of the device that holds the block, and -1 exactly where b >= hist_blocks. Every device holds exactly 2 blocks of each slice's requests. The blocks of the 4 requests of one ranker group lie on devices of one dev index (over all cuts) at most 1 times, and some group reaches 1. `slot_ids`: -1 exactly where owner_ids is -1; the blocks of all slices use every cache row of every device exactly once.
All inputs are finite; a program needn't handle non-finite values.
Results may differ from a plain program's by a relative error of at most 0.0046.
Values may be sent and summed in bfloat16 or wider, within the bound.
No kernel may reach another device: no remote copies, remote signals or barrier semaphores. Data moves between devices by JAX's collectives and lax.ppermute only.
A program may use at most 128 MiB of HBM per device.

v0:
```python
import jax
import jax.numpy as jnp
from jax import lax
from jax.sharding import PartitionSpec as P

H = 8
DH = 128
HB = 32
RQ = 4
TILE = 32


EPS = 1e-05


def ranked(selected, count):
    sequence = jnp.cumsum(selected.astype(jnp.int32), axis=-1) - 1
    picks = jnp.arange(count, dtype=jnp.int32)
    return selected[..., None, :] & (sequence[..., None, :] == picks[:, None])


def local(
    kv_cache,
    queries,
    gates,
    tokens,
    w_out,
    norm_gain,
    hist_blocks,
    ranker_list,
    owner_ids,
    slot_ids,
    block_mask,
):
    cut_count = lax.axis_size("cuts")
    dev_count = lax.axis_size("dev")
    this_cut = lax.axis_index("cuts")
    this_dev = lax.axis_index("dev")
    groups = dev_count // H
    group_index = this_dev % groups
    pool_size, block_items, width = kv_cache.shape
    slab_width = width // H
    head_size = slab_width // 2
    owned = pool_size // cut_count
    per_group = RQ * HB
    live_cut = owned * cut_count * dev_count
    capacity = (min(per_group, live_cut) + dev_count - 1) // dev_count
    request_count = ranker_list.shape[1]
    keys_cut = request_count * HB
    cut_rows = jnp.arange(cut_count)[:, None]
    owners_ranked = owner_ids[cut_rows, ranker_list].reshape(cut_count, keys_cut)
    slots_ranked = slot_ids[cut_rows, ranker_list].reshape(cut_count, keys_cut)
    owner_self = this_cut * dev_count + this_dev
    chosen = ranked(owners_ranked == owner_self, owned)
    send_rows = jnp.sum(jnp.where(chosen, slots_ranked[:, None, :], 0), axis=-1)
    packed = kv_cache[send_rows.reshape(-1)].reshape(cut_count, owned, block_items, width)
    arrived = lax.all_to_all(packed, "cuts", split_axis=0, concat_axis=0, tiled=True)
    owner_table = lax.dynamic_index_in_dim(owners_ranked, this_cut, 0, keepdims=False)
    sources = jnp.arange(cut_count, dtype=jnp.int32) * dev_count + this_dev
    relay_pick = ranked(owner_table[None, :] == sources[:, None], owned)
    key_index = jnp.arange(keys_cut, dtype=jnp.int32)
    key_of = jnp.sum(jnp.where(relay_pick, key_index, 0), axis=-1).reshape(pool_size)
    group_of = key_of // per_group
    sequence = jnp.arange(pool_size)
    earlier = (group_of[None, :] == group_of[:, None]) & (sequence[None, :] < sequence[:, None])
    target = group_of * capacity + jnp.sum(earlier, axis=1)
    heads_first = arrived.reshape(pool_size, block_items, H, slab_width).transpose(2, 0, 1, 3)
    outgoing = jnp.zeros((H, groups * capacity, block_items, slab_width), arrived.dtype)
    outgoing = (
        outgoing.at[:, target]
        .set(heads_first)
        .reshape(dev_count, capacity, block_items, slab_width)
    )
    received = lax.all_to_all(outgoing, "dev", split_axis=0, concat_axis=0, tiled=True)
    flat_blocks = received.reshape(dev_count * capacity, block_items, slab_width)
    cut_list = lax.dynamic_index_in_dim(ranker_list, this_cut, 0, keepdims=False)
    requests = lax.dynamic_slice_in_dim(cut_list, group_index * RQ, RQ)
    lengths = lax.dynamic_index_in_dim(hist_blocks, this_cut, 0, keepdims=False)[requests]
    group_mask = lax.dynamic_index_in_dim(block_mask, this_cut, 0, keepdims=False)[requests]
    live_blocks = jnp.arange(HB, dtype=jnp.int32)[None, :] < lengths[:, None]
    is_live = live_blocks.reshape(per_group)
    group_owners = lax.dynamic_slice_in_dim(owner_table, group_index * per_group, per_group)
    src_dev = group_owners % dev_count
    src_cut = group_owners // dev_count
    position = jnp.arange(per_group)
    before = (
        is_live[None, :]
        & (src_dev[None, :] == src_dev[:, None])
        & (
            (src_cut[None, :] < src_cut[:, None])
            | (src_cut[None, :] == src_cut[:, None]) & (position[None, :] < position[:, None])
        )
    )
    slot_of = jnp.where(is_live, src_dev * capacity + jnp.sum(before, axis=1), 0).reshape(RQ, HB)
    tile_mask = (group_mask * live_blocks[:, None, :].astype(jnp.int32)).astype(jnp.float32)
    query_all = queries.reshape(RQ, -1, head_size)

    def attend(query, slot_rows, tiles):
        blocks = flat_blocks[slot_rows]
        key_rows = blocks[:, :, :head_size].reshape(-1, head_size)
        value_rows = blocks[:, :, head_size:].reshape(-1, head_size)
        scores = jnp.einsum(
            "ce,ke->ck", query, key_rows, preferred_element_type=jnp.float32
        ) * DH ** (-0.5)
        allowed = jnp.repeat(tiles, TILE, axis=0)
        rows_here = query.shape[0]
        weights = jax.nn.silu(scores).reshape(rows_here, HB, block_items) * allowed[:, :, None]
        weights = weights.reshape(rows_here, -1).astype(jnp.bfloat16)
        return jnp.dot(weights, value_rows, preferred_element_type=jnp.float32).astype(jnp.bfloat16)

    attended = lax.map(
        lambda parts: attend(parts[0], parts[1], parts[2]), (query_all, slot_of, tile_mask)
    )
    rows_each = attended.shape[0] * attended.shape[1] // dev_count
    back = lax.all_to_all(
        attended.reshape(dev_count, rows_each, head_size),
        "dev",
        split_axis=0,
        concat_axis=0,
        tiled=True,
    )
    gathered = back.reshape(H, groups, rows_each, head_size).transpose(1, 2, 0, 3)
    gathered = gathered.reshape(groups * rows_each, H * head_size).astype(jnp.float32)
    row_mean = jnp.mean(gathered, axis=-1, keepdims=True)
    centred = gathered - row_mean
    variance = jnp.mean(centred * centred, axis=-1, keepdims=True)
    normed = centred * lax.rsqrt(variance + EPS) * norm_gain
    gate_rows = gates.reshape(-1, H * head_size).astype(jnp.float32)
    gated = (normed * jax.nn.silu(gate_rows)).astype(jnp.bfloat16)
    projected = jnp.dot(
        gated, lax.all_gather(w_out, "dev", axis=0, tiled=True), preferred_element_type=jnp.float32
    )
    return (tokens.astype(jnp.float32) + projected.reshape(tokens.shape)).astype(jnp.bfloat16)


def solution(mesh):
    return jax.shard_map(
        local,
        mesh=mesh,
        in_specs=(
            P(("cuts", "dev"), None, None),
            P("cuts", "dev", None, None),
            P("cuts", None, "dev", None),
            P("cuts", None, "dev", None),
            P("dev", None),
            P(),
            P(),
            P(),
            P(),
            P(),
            P(),
        ),
        out_specs=P("cuts", None, "dev", None),
        check_vma=False,
    )
```

profile of v0, /device:TPU:1, one launch (start us, length us, event | category | flops | bytes accessed | tf_op | source)
XLA Modules:
  0.0 462.8 jit_solution(12972533517419381463)
XLA Ops:
  6.5 0.7 fusion.49
  7.4 0.9 copy.49
  8.3 1.9 gather_fusion.2
  10.2 0.1 reshape.507
  10.4 1.2 reduce-window.16
  11.6 0.2 slice_reduce_fusion
  11.8 0.2 reduce-window.19
  12.1 0.9 copy.52
  13.1 1.9 gather_fusion.3
  15.0 0.1 broadcast_in_dim.40
  15.1 0.2 select_reduce_fusion
  15.3 0.1 copy.53
  15.5 5.0 %gather_fusion.4 = bf16[8,128,2048]{2,1,0:T(8,128)(2,1)} fusion(bf16[8,128,2048]{2,1,0:T(8,128)(2,1)} %param.13, s32[1024]{0:T(1024)S(1)} %pad_clamp_fusion.1), kind=kCustom, calls=%fused_computation.4 | custom fusion | bytes 8388640 | tf_op jit(solution)/shard_map/gather | solution.py:56
  20.4 6.4 %copy.54 = bf16[8,128,2048]{1,2,0:T(8,128)(2,1)} copy(bf16[8,128,2048]{2,1,0:T(8,128)(2,1)} %gather_fusion.4) | data formatting | bytes 8388608 | tf_op jit(solution)/shard_map/gather | solution.py:56
  26.9 4.8 %all-to-all-start = ((bf16[4,2,128,2048]{2,3,1,0:T(8,128)(2,1)}), bf16[4,2,128,2048]{2,3,1,0:T(8,128)(2,1)}, u32[]{:S(2)}, u32[]{:S(2)}) async-start(bf16[4,2,128,2048]{2,3,1,0:T(8,128)(2,1)} %bitcast.158), calls=%async_computation | async-start | bytes 8388608 | tf_op jit(solution)/shard_map/all_to_all | solution.py:57
  31.8 1.1 reduce-window.14
  33.0 0.2 slice_reduce_fusion.1
  33.2 0.2 reduce-window.15
  33.6 0.2 select_reduce_fusion.1
  34.0 0.2 convert_reduce_fusion.1
  34.2 40.8 %all-to-all-done = bf16[4,2,128,2048]{2,3,1,0:T(8,128)(2,1)} async-done(((bf16[4,2,128,2048]{2,3,1,0:T(8,128)(2,1)}), bf16[4,2,128,2048]{2,3,1,0:T(8,128)(2,1)}, u32[]{:S(2)}, u32[]{:S(2)}) %all-to-all-start) | async-done | bytes 4194336 | tf_op jit(solution)/shard_map/all_to_all | solution.py:57
  75.0 6.4 %copy.55 = bf16[8,8,128,256]{3,2,1,0:T(8,128)(2,1)} copy(bf16[8,8,128,256]{2,3,1,0:T(8,128)(2,1)} %bitcast.23) | data formatting | bytes 8388608 | tf_op jit(solution)/shard_map/transpose | solution.py:67
  81.5 4.3 broadcast_in_dim.37
  85.7 10.7 %scatter_fusion = bf16[8,16,128,256]{3,2,1,0:T(8,128)(2,1)} fusion(bf16[8,16,128,256]{3,2,1,0:T(8,128)(2,1)} %broadcast_in_dim.37, s32[8]{0:T(128)S(1)} %fusion.53, bf16[8,8,128,256]{3,2,1,0:T(8,128)(2,1)} %copy.55), kind=kCustom, calls=%fused_computation.6 | custom fusion | bytes 12582944 | tf_op jit(solution)/shard_map/scatter | solution.py:71
  96.5 24.7 %all-to-all-start.1 = ((bf16[128,1,128,256]{3,2,1,0:T(8,128)(2,1)}), bf16[128,1,128,256]{3,2,1,0:T(8,128)(2,1)}, u32[]{:S(2)}, u32[]{:S(2)}) async-start(bf16[128,1,128,256]{3,2,1,0:T(8,128)(2,1)} %bitcast.155), calls=%async_computation.1 | async-start | bytes 16777216 | tf_op jit(solution)/shard_map/all_to_all | solution.py:74
  121.2 0.2 all-gather.2.cloned.1.call-start
  121.4 0.5 all-gather.2.cloned.1.call-update
  122.0 0.1 copy.57
  122.2 0.8 fusion.52
  123.0 0.5 gather_fusion.5
  123.5 0.7 fusion.50
  124.2 0.6 gather_fusion.1
  125.0 0.5 broadcast.549
  125.6 0.7 fusion.58
  126.3 0.2 convert_reduce_fusion
  126.6 0.7 fusion.45
  127.3 212.5 %all-to-all-done.1 = bf16[128,1,128,256]{3,2,1,0:T(8,128)(2,1)} async-done(((bf16[128,1,128,256]{3,2,1,0:T(8,128)(2,1)}), bf16[128,1,128,256]{3,2,1,0:T(8,128)(2,1)}, u32[]{:S(2)}, u32[]{:S(2)}) %all-to-all-start.1) | async-done | bytes 8388640 | tf_op jit(solution)/shard_map/all_to_all | solution.py:74
  339.8 51.3 %while.10 = (s32[]{:T(128)}, bf16[4,192,128]{2,1,0:T(8,128)(2,1)}, bf16[4,192,128]{2,1,0:T(8,128)(2,1)}, s32[4,32]{1,0:T(4,128)}, bf16[128,128,256]{2,1,0:T(8,128)(2,1)}, /*index=5*/f32[4,6,32]{2,1,0:T(8,128)S(1)}, s32[]{:T(128)}) while((s32[]{:T(128)}, bf16[4,192,128]{2,1,0:T(8,128)(2,1)}, bf16[4,192,128]{2,1,0:T(8,128)(2,1)}, ...), condition=%wide.region_10.11_spmd, body=%wide.region_9.10_spmd.sunk | while | flops 408183904 | bytes 16932692 | solution.py:111
  339.8 0.7 fusion.71
  340.5 4.1 gather_fusion
  344.6 2.0 fusion.72
  346.6 0.9 mul.176
  347.4 5.2 %fusion.73 = bf16[4,192,128]{2,1,0:T(8,128)(2,1)} fusion(bf16[4,192,128]{2,1,0:T(8,128)(2,1)} %get-tuple-element.109, s32[]{:T(128)} %get-tuple-element.108, bf16[4096,128]{1,0:T(8,128)(2,1)} %bitcast.157, f32[24,8,32,128]{3,2,1,0:T(8,128)S(1)} %bitcast.154, bf16[4096,128]{1,0:T(8,128)(2,1)} %bitcast.156, bf16[4,192,128]{2,1,0:T(8,128)(2,1)} %get-tuple-element.117), kind=kOutput, calls=%fused_computation.13.clone.1 | convolution fusion | flops 408182784 | bytes 5342208 | tf_op jit(solution)/shard_map/while/body/eval_jaxpr/dot_general | solution.py:109
  352.6 0.7 fusion.71
  353.3 4.1 gather_fusion
  357.4 2.0 fusion.72
  359.4 0.9 mul.176
  360.3 5.2 %fusion.73 = bf16[4,192,128]{2,1,0:T(8,128)(2,1)} fusion(bf16[4,192,128]{2,1,0:T(8,128)(2,1)} %get-tuple-element.109, s32[]{:T(128)} %get-tuple-element.108, bf16[4096,128]{1,0:T(8,128)(2,1)} %bitcast.157, f32[24,8,32,128]{3,2,1,0:T(8,128)S(1)} %bitcast.154, bf16[4096,128]{1,0:T(8,128)(2,1)} %bitcast.156, bf16[4,192,128]{2,1,0:T(8,128)(2,1)} %get-tuple-element.117), kind=kOutput, calls=%fused_computation.13.clone.1 | convolution fusion | flops 408182784 | bytes 5342208 | tf_op jit(solution)/shard_map/while/body/eval_jaxpr/dot_general | solution.py:109
  365.4 0.7 fusion.71
  366.1 4.2 gather_fusion
  370.3 2.0 fusion.72
  372.3 0.9 mul.176
  373.2 5.2 %fusion.73 = bf16[4,192,128]{2,1,0:T(8,128)(2,1)} fusion(bf16[4,192,128]{2,1,0:T(8,128)(2,1)} %get-tuple-element.109, s32[]{:T(128)} %get-tuple-element.108, bf16[4096,128]{1,0:T(8,128)(2,1)} %bitcast.157, f32[24,8,32,128]{3,2,1,0:T(8,128)S(1)} %bitcast.154, bf16[4096,128]{1,0:T(8,128)(2,1)} %bitcast.156, bf16[4,192,128]{2,1,0:T(8,128)(2,1)} %get-tuple-element.117), kind=kOutput, calls=%fused_computation.13.clone.1 | convolution fusion | flops 408182784 | bytes 5342208 | tf_op jit(solution)/shard_map/while/body/eval_jaxpr/dot_general | solution.py:109
  378.3 0.7 fusion.71
  379.0 4.1 gather_fusion
  383.1 2.0 fusion.72
  385.1 0.9 mul.176
  386.0 5.2 %fusion.73 = bf16[4,192,128]{2,1,0:T(8,128)(2,1)} fusion(bf16[4,192,128]{2,1,0:T(8,128)(2,1)} %get-tuple-element.109, s32[]{:T(128)} %get-tuple-element.108, bf16[4096,128]{1,0:T(8,128)(2,1)} %bitcast.157, f32[24,8,32,128]{3,2,1,0:T(8,128)S(1)} %bitcast.154, bf16[4096,128]{1,0:T(8,128)(2,1)} %bitcast.156, bf16[4,192,128]{2,1,0:T(8,128)(2,1)} %get-tuple-element.117), kind=kOutput, calls=%fused_computation.13.clone.1 | convolution fusion | flops 408182784 | bytes 5342208 | tf_op jit(solution)/shard_map/while/body/eval_jaxpr/dot_general | solution.py:109
  391.2 1.0 reshape.517
  392.2 59.9 %all_to_all.15 = bf16[128,6,128]{2,1,0:T(8,128)(2,1)S(1)} all-to-all(bf16[128,6,128]{2,1,0:T(8,128)(2,1)S(1)} %reshape.517), channel_id=1, replica_groups=mesh['cuts'=4,'dev'=128] {'dev'}, dimensions={0} | all-to-all | bytes 393216 | tf_op jit(solution)/shard_map/all_to_all | solution.py:115
  452.1 0.1 fusion.31
  452.4 0.2 multiply_reduce_fusion
  452.8 0.2 copy.58
  453.1 2.9 fusion.23
  (58 shorter events, 1.8 us)
Async XLA Ops:
  6.5 115.5 %copy-start = (s32[4,64,6,32]{1,3,2,0:T(8,128)S(1)}, s32[4,64,6,32]{1,3,2,0:T(8,128)}, u32[]{:S(2)}) copy-start(s32[4,64,6,32]{1,3,2,0:T(8,128)} %param.23) | copy-start | bytes 589828
  26.9 48.1 %all-to-all-start = ((bf16[4,2,128,2048]{2,3,1,0:T(8,128)(2,1)}), bf16[4,2,128,2048]{2,3,1,0:T(8,128)(2,1)}, u32[]{:S(2)}, u32[]{:S(2)}) async-start(bf16[4,2,128,2048]{2,3,1,0:T(8,128)(2,1)} %bitcast.158), calls=%async_computation | async-start | bytes 8388608 | tf_op jit(solution)/shard_map/all_to_all | solution.py:57
  96.5 243.3 %all-to-all-start.1 = ((bf16[128,1,128,256]{3,2,1,0:T(8,128)(2,1)}), bf16[128,1,128,256]{3,2,1,0:T(8,128)(2,1)}, u32[]{:S(2)}, u32[]{:S(2)}) async-start(bf16[128,1,128,256]{3,2,1,0:T(8,128)(2,1)} %bitcast.155), calls=%async_computation.1 | async-start | bytes 16777216 | tf_op jit(solution)/shard_map/all_to_all | solution.py:74
  121.2 331.9 %all-gather.2.cloned.1.call-start = ((), (), s32[]{:S(2)}) async-start(), calls=%async_computation.3 | async-start | bytes 2113536 | tf_op jit(solution)/shard_map/all_gather | solution.py:131
  391.1 62.0 %copy-start.1 = (bf16[1,16,6,1024]{3,1,2,0:T(8,128)(2,1)S(1)}, bf16[1,16,6,1024]{3,1,2,0:T(8,128)(2,1)}, u32[]{:S(2)}) copy-start(bf16[1,16,6,1024]{3,1,2,0:T(8,128)(2,1)} %param.16) | copy-start | bytes 589828
  391.2 62.0 %copy-start.2 = (bf16[1,16,6,1024]{3,1,2,0:T(8,128)(2,1)S(1)}, bf16[1,16,6,1024]{3,1,2,0:T(8,128)(2,1)}, u32[]{:S(2)}) copy-start(bf16[1,16,6,1024]{3,1,2,0:T(8,128)(2,1)} %param.15) | copy-start | bytes 589828
  391.2 62.0 %copy-start.3 = (f32[1024]{0:T(1024)S(1)}, f32[1024]{0:T(1024)}, u32[]{:S(2)}) copy-start(f32[1024]{0:T(1024)} %param.18) | copy-start | bytes 12292
Sparse Core Ops, SparseCore 0:
  125.2 257.8 all-gather.1
where the time goes:
time: 468 us; the launch traced here: 463 us
  waiting for transfers between devices  254 us (54%)
  local copies, waits for them, and re-layouts  72.9 us (16%)
  blocking collectives  59.9 us (13%)
  starting transfers between devices  29.8 us (6%)
  matrix products  23.6 us (5%)
  between operations  13.7 us (3%)
  other arithmetic  9.14 us (2%)
    all_to_all x1, waiting for transfers between devices, local(): lax.all_to_all(outgoing, 'dev', split_axis=0, concat_axis=0, tiled=True)  213 us
    all_to_all x1, blocking collectives, local(): lax.all_to_all(attended.reshape(dev_count, rows_each, head_size), 'dev',...  59.9 us
    all_to_all x1, waiting for transfers between devices, local(): lax.all_to_all(packed, 'cuts', split_axis=0, concat_axis=0, tiled=True)  40.8 us
    all_to_all x1, starting transfers between devices, local(): lax.all_to_all(outgoing, 'dev', split_axis=0, concat_axis=0, tiled=True)  24.7 us
    dot_general x4, matrix products, attend(): jnp.dot(weights, value_rows, preferred_element_type=jnp.float32)  20.7 us
    gather x4, local copies, waits for them, and re-layouts, attend(): blocks = flat_blocks[slot_rows]  16.3 us
    gather x2, local copies, waits for them, and re-layouts, local(): kv_cache[send_rows.reshape(-1)]  11.4 us
    scatter x1, local copies, waits for them, and re-layouts, local(): outgoing = outgoing.at[:, target].set(heads_first).reshape(dev_count, cap...  10.7 us
  transfers between devices with their start and end apart: 3, of which 2 were waited for; matrix products, arithmetic and copies ran while one was open for 13% of the time, Pallas kernels for 0%

commit v1 on v0

v1 whole, which is shorter than its diff:
```python
import jax
import jax.numpy as jnp
from jax import lax
from jax.experimental import pallas as pl
from jax.experimental.pallas import tpu as pltpu
from jax.sharding import Mesh, PartitionSpec as P

H = 8
DH = 128
HB = 32
RQ = 4
TILE = 32
BLK = 128
CUTS, ZS, YS, CORES = 4, 8, 8, 2
GROUPS = 16
REQUESTS = 64
CAND = 192
CT = 6
ROWS_G = RQ * CAND
OWN = 2
SLAB = 2 * DH
PIECE = 6
SOURCES = CUTS * ZS
BLOCKS_HERE = SOURCES * OWN
KV_STEP = 8
EPS = 1e-05


def pack_kernel(self_ref, owner_ref, slot_ref, kv_ref, out_ref, held, in_sems, out_sems):
    me = self_ref[0]
    rows = lax.broadcasted_iota(jnp.int32, (REQUESTS, HB), 0)
    blocks = lax.broadcasted_iota(jnp.int32, (REQUESTS, HB), 1)
    place = (rows * HB + blocks) * 8
    fetches = []
    for cut in range(CUTS):
        mine = owner_ref[cut] == me
        code = place + slot_ref[cut]
        first = jnp.min(jnp.where(mine, code, REQUESTS * HB * 8 - 1))
        last = jnp.max(jnp.where(mine, code, 0))
        for own, found in enumerate((first, last)):
            i = cut * OWN + own
            fetch = pltpu.make_async_copy(kv_ref.at[found & 7], held.at[i], in_sems.at[i])
            fetch.start()
            fetches.append(fetch)
    stores = []
    for i, fetch in enumerate(fetches):
        fetch.wait()
        for head in range(H):
            store = pltpu.make_async_copy(
                held.at[i, :, pl.ds(head * SLAB, SLAB)],
                out_ref.at[(i // OWN) * H + head, i % OWN],
                out_sems.at[i * H + head],
            )
            store.start()
            stores.append(store)
    for store in stores:
        store.wait()


def pack(me, owner_ids, slot_ids, kv_cache):
    count = CUTS * OWN
    return pl.pallas_call(
        pack_kernel,
        out_shape=jax.ShapeDtypeStruct((SOURCES, OWN, BLK, SLAB), kv_cache.dtype),
        in_specs=[
            pl.BlockSpec(memory_space=pltpu.SMEM),
            pl.BlockSpec(memory_space=pltpu.VMEM),
            pl.BlockSpec(memory_space=pltpu.VMEM),
            pl.BlockSpec(memory_space=pl.ANY),
        ],
        out_specs=pl.BlockSpec(memory_space=pl.ANY),
        scratch_shapes=[
            pltpu.VMEM((count, BLK, H * SLAB), kv_cache.dtype),
            pltpu.SemaphoreType.DMA((count,)),
            pltpu.SemaphoreType.DMA((count * H,)),
        ],
        compiler_params=pltpu.CompilerParams(vmem_limit_bytes=24 << 20),
    )(me.reshape(1), owner_ids, slot_ids, kv_cache)


def attend_kernel(pos_ref, core_ref, mask_ref, q_ref, kv_ref, keep_ref, send_ref, acc_ref):
    step = pl.program_id(0)

    @pl.when(step == 0)
    def _():
        def clear(i, carry):
            acc_ref[pl.ds(pl.multiple_of(i * CAND, CAND), CAND), :] = jnp.zeros((CAND, DH), jnp.float32)
            return carry

        lax.fori_loop(0, REQUESTS, clear, 0)

    for u in range(KV_STEP):
        block = step * KV_STEP + u
        rows = pl.ds(pl.multiple_of(pos_ref[block] * CAND, CAND), CAND)
        query = q_ref[rows, :]
        scores = lax.dot_general(
            query, kv_ref[u, :, :DH], (((1,), (1,)), ((), ())), preferred_element_type=jnp.float32
        )
        half = scores * (0.5 * DH ** (-0.5))
        silu = half + half * jnp.tanh(half)
        weights = jnp.concatenate(
            [
                (silu[t * TILE : (t + 1) * TILE] * mask_ref[block * CT + t]).astype(jnp.bfloat16)
                for t in range(CT)
            ],
            axis=0,
        )
        acc_ref[rows, :] += jnp.dot(weights, kv_ref[u, :, DH:], preferred_element_type=jnp.float32)

    @pl.when(step == BLOCKS_HERE // KV_STEP - 1)
    def _():
        core = core_ref[0]

        def split(target, carry):
            base = target * (CORES * PIECE)
            for r in range(PIECE):
                for ref, side in ((keep_ref, core), (send_ref, 1 - core)):
                    first = base + side * PIECE + r
                    ref[target, pl.ds(r * GROUPS, GROUPS), :] = acc_ref[
                        pl.ds(first, GROUPS, stride=ROWS_G), :
                    ].astype(ref.dtype)
            return carry

        lax.fori_loop(0, ZS * YS, split, 0)


def attend(positions, core, masks, queries, blocks):
    piece = jax.ShapeDtypeStruct((ZS * YS, GROUPS * PIECE, DH), jnp.bfloat16)
    whole = pl.BlockSpec((ZS * YS, GROUPS * PIECE, DH), lambda i, *_: (0, 0, 0))
    flops = 4 * BLOCKS_HERE * CAND * BLK * DH
    return pl.pallas_call(
        attend_kernel,
        out_shape=(piece, piece),
        grid_spec=pltpu.PrefetchScalarGridSpec(
            num_scalar_prefetch=3,
            grid=(BLOCKS_HERE // KV_STEP,),
            in_specs=[
                pl.BlockSpec((REQUESTS * CAND, DH), lambda i, *_: (0, 0)),
                pl.BlockSpec((KV_STEP, BLK, SLAB), lambda i, *_: (i, 0, 0)),
            ],
            out_specs=(whole, whole),
            scratch_shapes=[pltpu.VMEM((REQUESTS * CAND, DH), jnp.float32)],
        ),
        compiler_params=pltpu.CompilerParams(
            vmem_limit_bytes=40 << 20, dimension_semantics=("arbitrary",)
        ),
        cost_estimate=pl.CostEstimate(
            flops=flops, bytes_accessed=10 << 20, transcendentals=BLOCKS_HERE * CAND * BLK
        ),
    )(positions, core, masks, queries, blocks)


def finish_kernel(back_ref, gain_ref, gate_ref, token_ref, w_ref, out_ref):
    heads = []
    for head in range(H):
        total = back_ref[head * YS].astype(jnp.float32)
        for y in range(1, YS):
            total = total + back_ref[head * YS + y].astype(jnp.float32)
        heads.append(total.astype(jnp.bfloat16).astype(jnp.float32))
    rows = jnp.concatenate(heads, axis=1)
    centred = rows - jnp.mean(rows, axis=-1, keepdims=True)
    variance = jnp.mean(centred * centred, axis=-1, keepdims=True)
    normed = centred * lax.rsqrt(variance + EPS) * gain_ref[...]
    gate = gate_ref[...].astype(jnp.float32)
    gated = (normed * (gate * jax.nn.sigmoid(gate))).astype(jnp.bfloat16)
    projected = jnp.dot(gated, w_ref[...], preferred_element_type=jnp.float32)
    out_ref[...] = (token_ref[...].astype(jnp.float32) + projected).astype(out_ref.dtype)


def finish(back, gain, gate_rows, token_rows, w_all):
    return pl.pallas_call(
        finish_kernel,
        out_shape=jax.ShapeDtypeStruct(token_rows.shape, token_rows.dtype),
        in_specs=[pl.BlockSpec(memory_space=pltpu.VMEM)] * 5,
        out_specs=pl.BlockSpec(memory_space=pltpu.VMEM),
        compiler_params=pltpu.CompilerParams(vmem_limit_bytes=24 << 20),
    )(back, gain, gate_rows, token_rows, w_all)


def describe(cut, yc, hist_blocks, ranker_list, owner_ids, block_mask):
    owners = lax.dynamic_index_in_dim(owner_ids, cut, 0, keepdims=False).reshape(-1)
    ranking = lax.dynamic_index_in_dim(ranker_list, cut, 0, keepdims=False)
    lengths = lax.dynamic_index_in_dim(hist_blocks, cut, 0, keepdims=False)
    tiles = lax.dynamic_index_in_dim(block_mask, cut, 0, keepdims=False)
    source = jnp.arange(SOURCES, dtype=jnp.int32)
    source = (source // ZS) * (ZS * YS * CORES) + (source % ZS) * (YS * CORES) + yc
    found = owners[None, :] == source[:, None]
    place = jnp.arange(REQUESTS * HB, dtype=jnp.int32)[None, :]
    first = jnp.min(jnp.where(found, place, REQUESTS * HB - 1), axis=1)
    last = jnp.max(jnp.where(found, place, 0), axis=1)
    places = jnp.stack([first, last], axis=1).reshape(-1)
    request, block = places // HB, places % HB
    slots = jnp.arange(REQUESTS, dtype=jnp.int32)
    positions = jnp.sum(jnp.where(ranking[None, :] == request[:, None], slots[None, :], 0), axis=1)
    live = (block < lengths[request]).astype(jnp.float32)
    masks = tiles[request, :, block].astype(jnp.float32) * live[:, None]
    return positions, masks.reshape(-1)


def local(
    kv_cache,
    queries,
    gates,
    tokens,
    w_out,
    norm_gain,
    hist_blocks,
    ranker_list,
    owner_ids,
    slot_ids,
    block_mask,
):
    cut = lax.axis_index("cuts")
    core = lax.axis_index("core")
    me = lax.axis_index(("cuts", "z", "y", "core"))
    yc = lax.axis_index(("y", "core"))
    packed = pack(me, owner_ids, slot_ids, kv_cache)
    arrived = lax.all_to_all(packed, ("cuts", "z"), split_axis=0, concat_axis=0, tiled=True)
    query_all = lax.all_gather(queries.reshape(ROWS_G, DH), ("y", "core"), axis=0, tiled=True)
    w_all = lax.all_gather(w_out, ("z", "y", "core"), axis=0, tiled=True)
    positions, masks = describe(cut, yc, hist_blocks, ranker_list, owner_ids, block_mask)
    keep, send = attend(
        positions, core.reshape(1), masks, query_all, arrived.reshape(BLOCKS_HERE, BLK, SLAB)
    )
    other = lax.ppermute(send, "core", [(0, 1), (1, 0)])
    both = (keep.astype(jnp.float32) + other.astype(jnp.float32)).astype(jnp.bfloat16)
    back = lax.all_to_all(both, ("z", "y"), split_axis=0, concat_axis=0, tiled=True)
    width = H * DH
    gate_rows = gates.reshape(GROUPS, PIECE, width).transpose(1, 0, 2).reshape(-1, width)
    token_rows = tokens.reshape(GROUPS, PIECE, width).transpose(1, 0, 2).reshape(-1, width)
    mixed = finish(back, norm_gain.reshape(1, width), gate_rows, token_rows, w_all)
    return mixed.reshape(PIECE, GROUPS, width).transpose(1, 0, 2).reshape(tokens.shape)


def solution(mesh):
    grid = Mesh(
        mesh.devices.reshape(CUTS, ZS, YS, CORES), ("cuts", "z", "y", "core")
    )
    dev = ("z", "y", "core")
    return jax.shard_map(
        local,
        mesh=grid,
        in_specs=(
            P(("cuts",) + dev, None, None),
            P("cuts", dev, None, None),
            P("cuts", None, dev, None),
            P("cuts", None, dev, None),
            P(dev, None),
            P(),
            P(),
            P(),
            P(),
            P(),
            P(),
        ),
        out_specs=P("cuts", None, dev, None),
        check_vma=False,
    )
```

time: 468 us -> 265 us (0.57); the launches traced: 463 us -> 265 us
  waiting for transfers between devices: 254 us -> 182 us
  blocking collectives: 59.9 us -> 0 us
  local copies, waits for them, and re-layouts: 72.9 us -> 14.9 us
  matrix products: 23.6 us -> 0 us
  Pallas kernels: 0 us -> 20.7 us
  other arithmetic: 9.14 us -> 3.52 us
    all_to_all x2, waiting for transfers between devices: 253 us -> 44.4 us  [the longest x1 44.4 us: local(): lax.all_to_all(packed, ('cuts', 'z'), split_axis=0, concat_axis=0, tiled=...]
    all_gather x1 -> x2, waiting for transfers between devices: 0.02 us -> 133 us  [the longest x1 91.7 us: local(): w_all = lax.all_gather(w_out, ('z', 'y', 'core'), axis=0, tiled=True)]
    all_to_all x1 -> x0, blocking collectives: 59.9 us -> none  [local(): lax.all_to_all(attended.reshape(dev_count, rows_each, head_size), 'dev',...]
    gather x10 -> x2, local copies, waits for them, and re-layouts: 32.7 us -> 1.66 us  [the longest x1 0.88 us: describe(): masks = tiles[request, :, block].astype(jnp.float32) * live[:, None]]
    dot_general x5 -> x0, matrix products: 23.6 us -> none  [the longest x4 20.7 us: attend(): jnp.dot(weights, value_rows, preferred_element_type=jnp.float32)]
    pallas_call x0 -> x3, Pallas kernels: none -> 20.7 us  [the longest x1 16.7 us: attend(): pl.pallas_call(attend_kernel, out_shape=(piece, piece), grid_spec=pltpu.P...]
    scatter x1 -> x0, local copies, waits for them, and re-layouts: 10.7 us -> none  [local(): outgoing = outgoing.at[:, target].set(heads_first).reshape(dev_count, cap...]
    slice x5 -> x0, local copies, waits for them, and re-layouts: 8.21 us -> none  [the longest x4 7.99 us: attend(): key_rows = blocks[:, :, :head_size].reshape(-1, head_size)]
  transfers between devices with their start and end apart: 3 -> 5, of which waited for: 2 -> 4; matrix products, arithmetic and copies ran while one was open for 13% -> 3% of each run, Pallas kernels for 0% -> 0%
where the time goes in v1:
time: 265 us
  waiting for transfers between devices  182 us (69%)
  starting transfers between devices  29.2 us (11%)
  Pallas kernels  20.7 us (8%)
  between operations  15 us (6%)
  local copies, waits for them, and re-layouts  14.9 us (6%)
  other arithmetic  3.52 us (1%)
    all_gather x1, waiting for transfers between devices, local(): w_all = lax.all_gather(w_out, ('z', 'y', 'core'), axis=0, tiled=True)  91.7 us
    all_to_all x1, waiting for transfers between devices, local(): lax.all_to_all(packed, ('cuts', 'z'), split_axis=0, concat_axis=0, tiled=...  44.4 us
    all_gather x1, waiting for transfers between devices, local(): lax.all_gather(queries.reshape(ROWS_G, DH), ('y', 'core'), axis=0, tiled=...  41.7 us
    pallas_call x1, Pallas kernels, attend(): pl.pallas_call(attend_kernel, out_shape=(piece, piece), grid_spec=pltpu.P...  16.7 us
    all_to_all x1, starting transfers between devices, local(): lax.all_to_all(packed, ('cuts', 'z'), split_axis=0, concat_axis=0, tiled=...  13.8 us
    unnamed x18, local copies, waits for them, and re-layouts  9.56 us
    all_to_all x1, starting transfers between devices, local(): lax.all_to_all(both, ('z', 'y'), split_axis=0, concat_axis=0, tiled=True)  7.97 us
    ppermute x1, starting transfers between devices, local(): other = lax.ppermute(send, 'core', [(0, 1), (1, 0)])  7.28 us
  transfers between devices with their start and end apart: 5, of which 4 were waited for; matrix products, arithmetic and copies ran while one was open for 3% of the time, Pallas kernels for 0%

profile of v1, /device:TPU:1, one launch (start us, length us, event | category | flops | bytes accessed | tf_op | source)
XLA Modules:
  0.0 264.9 jit_solution(3076806866610986010)
XLA Ops:
  7.4 0.0 copy-start
  7.4 1.0 copy.27.owner_ref
  8.4 0.9 copy.28.slot_ref
  9.3 0.0 copy-start.2
  9.3 2.2 copy-done.2
  11.5 2.5 shard_map.109
  14.0 0.0 copy-start.1
  14.0 2.0 copy-done.1
  16.0 13.8 %all-to-all-start = ((bf16[32,2,128,256]{3,2,1,0:T(8,128)(2,1)}), bf16[32,2,128,256]{3,2,1,0:T(8,128)(2,1)}, u32[]{:S(2)}, u32[]{:S(2)}) async-start(bf16[32,2,128,256]{3,2,1,0:T(8,128)(2,1)} %copy-done.1), calls=%async_computation | async-start | bytes 8388608 | tf_op jit(solution)/shard_map/all_to_all | solution.py:218
  29.9 0.0 all-gather.6.cloned.1.call-start
  29.9 0.7 all-gather.6.cloned.1.call-update
  30.6 0.0 all-gather.4.cloned.1.call-start
  30.7 0.7 constant_dynamic-slice_fusion.2
  31.4 0.1 copy.23
  31.5 0.1 eq.36
  31.5 0.2 fusion
  31.8 0.1 copy.24
  31.9 0.1 reshape.211
  32.0 0.1 reshape.209
  32.1 0.0 copy-done
  32.1 0.9 copy.25
  33.1 0.7 fusion.6
  33.8 0.8 gather_fusion.1
  34.6 0.9 gather_fusion
  35.5 0.1 convert_multiply_fusion
  35.6 0.1 mul.49.mask_ref
  35.7 0.7 fusion.5
  36.4 0.2 select_reduce_fusion.pos_ref
  36.6 41.7 %all-gather.6.cloned.1.call-done = bf16[1,1,12288,128]{3,2,1,0:T(8,128)(2,1)} async-done(((bf16[1,1,768,128]{3,2,1,0:T(8,128)(2,1)}), bf16[1,1,12288,128]{3,2,1,0:T(8,128)(2,1)}) %all-gather.6.cloned.1.call-update) | async-done | bytes 3145744 | tf_op jit(solution)/shard_map/all_gather | solution.py:219
  78.3 44.4 %all-to-all-done = bf16[32,2,128,256]{3,2,1,0:T(8,128)(2,1)} async-done(((bf16[32,2,128,256]{3,2,1,0:T(8,128)(2,1)}), bf16[32,2,128,256]{3,2,1,0:T(8,128)(2,1)}, u32[]{:S(2)}, u32[]{:S(2)}) %all-to-all-start) | async-done | bytes 4194336 | tf_op jit(solution)/shard_map/all_to_all | solution.py:218
  122.6 0.0 copy-start.3
  122.6 1.9 copy-done.3
  124.5 16.7 %shard_map.110 = (bf16[64,96,128]{2,1,0:T(8,128)(2,1)S(1)}, bf16[64,96,128]{2,1,0:T(8,128)(2,1)S(1)}) custom-call(s32[64]{0:T(128)S(1)} %select_reduce_fusion.pos_ref, s32[1]{0:T(128)} %bitcast.3.core_ref, f32[384]{0:T(512)S(1)} %mul.49.mask_ref, bf16[12288,128]{1,0:T(8,128)(2,1)S(1)} %bitcast.30, bf16[64,128,256]{2,1,0:T(8,128)(2,1)} %bitcast.10.kv_ref), custom_call_target="tpu_custom_call" | custom-call | flops 805306368 | bytes 10485760 | tf_op jit(solution)/shard_map/pallas_call | solution.py:131
  141.2 7.3 %collective-permute-start = (bf16[64,96,128]{2,1,0:T(8,128)(2,1)S(1)}, bf16[64,96,128]{2,1,0:T(8,128)(2,1)}, u32[]{:S(2)}, u32[]{:S(2)}) collective-permute-start(bf16[64,96,128]{2,1,0:T(8,128)(2,1)S(1)} %get-tuple-element.8), channel_id=1, source_target_pairs={{0,1},{1,0},{2,3},{3,2},{4,5},{5,4},{6,7},{7,6},{8,9},{9,8},{10,11... | collective-permute-start | bytes 4718600 | tf_op jit(solution)/shard_map/ppermute | solution.py:225
  148.5 0.0 all-gather.4.cloned.1.call-update
  148.5 3.1 %collective-permute-done = bf16[64,96,128]{2,1,0:T(8,128)(2,1)} collective-permute-done((bf16[64,96,128]{2,1,0:T(8,128)(2,1)S(1)}, bf16[64,96,128]{2,1,0:T(8,128)(2,1)}, u32[]{:S(2)}, u32[]{:S(2)}) %collective-permute-start) | collective-permute-done | bytes 1572896 | tf_op jit(solution)/shard_map/ppermute | solution.py:225
  151.7 3.0 %add_convert_fusion = bf16[64,96,128]{2,1,0:T(8,128)(2,1)} fusion(bf16[64,96,128]{2,1,0:T(8,128)(2,1)} %collective-permute-done, bf16[64,96,128]{2,1,0:T(8,128)(2,1)S(1)} %get-tuple-element.7), kind=kLoop, calls=%fused_computation.2 | loop fusion | flops 3145728 | bytes 4718592 | tf_op jit(solution)/shard_map/convert_element_type | solution.py:226
  154.6 0.0 copy-start.5
  154.6 0.0 copy-start.6
  154.6 0.0 copy-start.7
  154.6 8.0 %all-to-all-start.1 = ((bf16[64,96,128]{2,1,0:T(8,128)(2,1)}), bf16[64,96,128]{2,1,0:T(8,128)(2,1)S(1)}, u32[]{:S(2)}, u32[]{:S(2)}) async-start(bf16[64,96,128]{2,1,0:T(8,128)(2,1)} %add_convert_fusion), calls=%async_computation.1 | async-start | bytes 3145728 | tf_op jit(solution)/shard_map/all_to_all | solution.py:227
  162.6 91.7 %all-gather.4.cloned.1.call-done.w_ref = bf16[1024,1024]{1,0:T(8,128)(2,1)} async-done(((bf16[8,1024]{1,0:T(8,128)(2,1)}), bf16[1024,1024]{1,0:T(8,128)(2,1)}) %all-gather.4.cloned.1.call-update) | async-done | bytes 2097168 | tf_op jit(solution)/shard_map/all_gather | solution.py:220
  254.3 0.0 all-to-all-done.1.back_ref
  254.3 0.0 copy-done.5
  254.3 0.0 copy-done.6
  254.3 0.0 copy-done.7
  254.3 0.0 copy-start.4
  254.4 1.6 copy-done.4
  255.9 1.5 shard_map.111
  (7 shorter events, 0.1 us)
Async XLA Ops:
  7.4 24.7 %copy-start = (s32[4,64,6,32]{1,3,2,0:T(8,128)S(1)}, s32[4,64,6,32]{1,3,2,0:T(8,128)}, u32[]{:S(2)}) copy-start(s32[4,64,6,32]{1,3,2,0:T(8,128)} %param.21) | copy-start | bytes 589828
  9.3 2.2 copy-start.2
  14.0 2.0 copy-start.1
  16.0 106.6 %all-to-all-start = ((bf16[32,2,128,256]{3,2,1,0:T(8,128)(2,1)}), bf16[32,2,128,256]{3,2,1,0:T(8,128)(2,1)}, u32[]{:S(2)}, u32[]{:S(2)}) async-start(bf16[32,2,128,256]{3,2,1,0:T(8,128)(2,1)} %copy-done.1), calls=%async_computation | async-start | bytes 8388608 | tf_op jit(solution)/shard_map/all_to_all | solution.py:218
  29.9 48.4 %all-gather.6.cloned.1.call-start = ((), (), s32[]{:S(2)}) async-start(), calls=%async_computation.3 | async-start | bytes 3342336 | tf_op jit(solution)/shard_map/all_gather | solution.py:219
  30.6 223.7 %all-gather.4.cloned.1.call-start = ((), (), s32[]{:S(2)}) async-start(), calls=%async_computation.2 | async-start | bytes 2113536 | tf_op jit(solution)/shard_map/all_gather | solution.py:220
  122.6 1.9 copy-start.3
  141.2 10.4 %collective-permute-start = (bf16[64,96,128]{2,1,0:T(8,128)(2,1)S(1)}, bf16[64,96,128]{2,1,0:T(8,128)(2,1)}, u32[]{:S(2)}, u32[]{:S(2)}) collective-permute-start(bf16[64,96,128]{2,1,0:T(8,128)(2,1)S(1)} %get-tuple-element.8), channel_id=1, source_target_pairs={{0,1},{1,0},{2,3},{3,2},{4,5},{5,4},{6,7},{7,6},{8,9},{9,8},{10,11... | collective-permute-start | bytes 4718600 | tf_op jit(solution)/shard_map/ppermute | solution.py:225
  154.6 99.7 %copy-start.5 = (bf16[1,16,6,1024]{3,1,2,0:T(8,128)(2,1)S(1)}, bf16[1,16,6,1024]{3,1,2,0:T(8,128)(2,1)}, u32[]{:S(2)}) copy-start(bf16[1,16,6,1024]{3,1,2,0:T(8,128)(2,1)} %param.13) | copy-start | bytes 589828
  154.6 99.7 %copy-start.6 = (bf16[1,16,6,1024]{3,1,2,0:T(8,128)(2,1)S(1)}, bf16[1,16,6,1024]{3,1,2,0:T(8,128)(2,1)}, u32[]{:S(2)}) copy-start(bf16[1,16,6,1024]{3,1,2,0:T(8,128)(2,1)} %param.14) | copy-start | bytes 589828
  154.6 99.7 %copy-start.7 = (f32[1024]{0:T(1024)S(1)}, f32[1024]{0:T(1024)}, u32[]{:S(2)}) copy-start(f32[1024]{0:T(1024)} %param.16) | copy-start | bytes 12292
  154.6 99.7 %all-to-all-start.1 = ((bf16[64,96,128]{2,1,0:T(8,128)(2,1)}), bf16[64,96,128]{2,1,0:T(8,128)(2,1)S(1)}, u32[]{:S(2)}, u32[]{:S(2)}) async-start(bf16[64,96,128]{2,1,0:T(8,128)(2,1)} %add_convert_fusion), calls=%async_computation.1 | async-start | bytes 3145728 | tf_op jit(solution)/shard_map/all_to_all | solution.py:227
  254.3 1.6 copy-start.4
Sparse Core Ops, SparseCore 0:
  32.8 45.3 all-gather.5
Sparse Core Ops, SparseCore 1:
  148.6 105.6 all-gather.3

commit v2 on v1

--- a/solution.py
+++ b/solution.py
@@ -24,12 +24,22 @@
 BLOCKS_HERE = SOURCES * OWN
 KV_STEP = 8
 EPS = 1e-05
-
-
-def pack_kernel(self_ref, owner_ref, slot_ref, kv_ref, out_ref, held, in_sems, out_sems):
+W_ROWS = 64
+PAYLOAD = ROWS_G + W_ROWS
+
+
+def pack_kernel(self_ref, owner_hbm, slot_hbm, kv_ref, out_ref, owner_ref, slot_ref, held, sems, in_sems, out_sems):
     me = self_ref[0]
-    rows = lax.broadcasted_iota(jnp.int32, (REQUESTS, HB), 0)
-    blocks = lax.broadcasted_iota(jnp.int32, (REQUESTS, HB), 1)
+    tables = [
+        pltpu.make_async_copy(owner_hbm, owner_ref, sems.at[0]),
+        pltpu.make_async_copy(slot_hbm, slot_ref, sems.at[1]),
+    ]
+    for table in tables:
+        table.start()
+    for table in tables:
+        table.wait()
+    blocks = lax.broadcasted_iota(jnp.int32, (HB, REQUESTS), 0)
+    rows = lax.broadcasted_iota(jnp.int32, (HB, REQUESTS), 1)
     place = (rows * HB + blocks) * 8
     fetches = []
     for cut in range(CUTS):
@@ -59,95 +69,126 @@
 
 def pack(me, owner_ids, slot_ids, kv_cache):
     count = CUTS * OWN
+    owner_ids, slot_ids = owner_ids.transpose(0, 2, 1), slot_ids.transpose(0, 2, 1)
     return pl.pallas_call(
         pack_kernel,
         out_shape=jax.ShapeDtypeStruct((SOURCES, OWN, BLK, SLAB), kv_cache.dtype),
         in_specs=[
             pl.BlockSpec(memory_space=pltpu.SMEM),
-            pl.BlockSpec(memory_space=pltpu.VMEM),
-            pl.BlockSpec(memory_space=pltpu.VMEM),
-            pl.BlockSpec(memory_space=pl.ANY),
+            pl.BlockSpec(memory_space=pltpu.HBM),
+            pl.BlockSpec(memory_space=pltpu.HBM),
+            pl.BlockSpec(memory_space=pltpu.HBM),
         ],
-        out_specs=pl.BlockSpec(memory_space=pl.ANY),
+        out_specs=pl.BlockSpec(memory_space=pltpu.HBM),
         scratch_shapes=[
+            pltpu.VMEM(owner_ids.shape, jnp.int32),
+            pltpu.VMEM(slot_ids.shape, jnp.int32),
             pltpu.VMEM((count, BLK, H * SLAB), kv_cache.dtype),
+            pltpu.SemaphoreType.DMA((2,)),
             pltpu.SemaphoreType.DMA((count,)),
             pltpu.SemaphoreType.DMA((count * H,)),
         ],
-        compiler_params=pltpu.CompilerParams(vmem_limit_bytes=24 << 20),
+        compiler_params=pltpu.CompilerParams(vmem_limit_bytes=60 << 20),
     )(me.reshape(1), owner_ids, slot_ids, kv_cache)
 
 
-def attend_kernel(pos_ref, core_ref, mask_ref, q_ref, kv_ref, keep_ref, send_ref, acc_ref):
-    step = pl.program_id(0)
-
-    @pl.when(step == 0)
-    def _():
-        def clear(i, carry):
-            acc_ref[pl.ds(pl.multiple_of(i * CAND, CAND), CAND), :] = jnp.zeros((CAND, DH), jnp.float32)
+def attend_kernel(
+    pos_ref, core_ref, mask_ref, q_hbm, kv_hbm, keep_hbm, send_hbm, q_ref, kv_ref, acc_ref, keep_ref, send_ref, q_sems, in_sems, out_sems
+):
+    steps = BLOCKS_HERE // KV_STEP
+
+    def fetch(step):
+        part = pl.ds(step * KV_STEP, KV_STEP)
+        return pltpu.make_async_copy(kv_hbm.at[part], kv_ref.at[part], in_sems.at[step])
+
+    asked = []
+    for group in range(GROUPS):
+        asked.append(pltpu.make_async_copy(q_hbm.at[group, pl.ds(0, ROWS_G)], q_ref.at[group], q_sems.at[group]))
+        asked[-1].start()
+    for step in range(steps):
+        fetch(step).start()
+
+    def clear(i, carry):
+        acc_ref[pl.ds(pl.multiple_of(i * CAND, CAND), CAND), :] = jnp.zeros((CAND, DH), jnp.float32)
+        return carry
+
+    lax.fori_loop(0, REQUESTS, clear, 0, unroll=4)
+    for copy in asked:
+        copy.wait()
+
+    def work(step, carry):
+        fetch(step).wait()
+        parts = []
+        for u in range(KV_STEP):
+            block = step * KV_STEP + u
+            place = pos_ref[block]
+            query = q_ref[place >> 2, pl.ds(pl.multiple_of((place & 3) * CAND, CAND), CAND), :]
+            keys = kv_ref[block, :, :DH].astype(jnp.float32).T.astype(jnp.bfloat16)
+            scores = jnp.dot(query, keys, preferred_element_type=jnp.float32)
+            half = scores * (0.5 * DH ** (-0.5))
+            silu = half + half * jnp.tanh(half)
+            weights = jnp.concatenate(
+                [
+                    (silu[t * TILE : (t + 1) * TILE] * mask_ref[block * CT + t]).astype(jnp.bfloat16)
+                    for t in range(CT)
+                ],
+                axis=0,
+            )
+            parts.append(jnp.dot(weights, kv_ref[block, :, DH:], preferred_element_type=jnp.float32))
+        for u in range(KV_STEP):
+            rows = pl.ds(pl.multiple_of(pos_ref[step * KV_STEP + u] * CAND, CAND), CAND)
+            acc_ref[rows, :] += parts[u]
+        return carry
+
+    lax.fori_loop(0, steps, work, 0)
+
+    core = core_ref[0]
+    copies = []
+    for out, (ref, hbm, side) in enumerate(((send_ref, send_hbm, 1 - core), (keep_ref, keep_hbm, core))):
+
+        def split(target, carry):
+            first = target * (CORES * PIECE) + side * PIECE
+            for r in range(PIECE):
+                ref[target, pl.ds(r * GROUPS, GROUPS), :] = acc_ref[
+                    pl.ds(first + r, GROUPS, stride=ROWS_G), :
+                ].astype(ref.dtype)
             return carry
 
-        lax.fori_loop(0, REQUESTS, clear, 0)
-
-    for u in range(KV_STEP):
-        block = step * KV_STEP + u
-        rows = pl.ds(pl.multiple_of(pos_ref[block] * CAND, CAND), CAND)
-        query = q_ref[rows, :]
-        scores = lax.dot_general(
-            query, kv_ref[u, :, :DH], (((1,), (1,)), ((), ())), preferred_element_type=jnp.float32
-        )
-        half = scores * (0.5 * DH ** (-0.5))
-        silu = half + half * jnp.tanh(half)
-        weights = jnp.concatenate(
-            [
-                (silu[t * TILE : (t + 1) * TILE] * mask_ref[block * CT + t]).astype(jnp.bfloat16)
-                for t in range(CT)
-            ],
-            axis=0,
-        )
-        acc_ref[rows, :] += jnp.dot(weights, kv_ref[u, :, DH:], preferred_element_type=jnp.float32)
-
-    @pl.when(step == BLOCKS_HERE // KV_STEP - 1)
-    def _():
-        core = core_ref[0]
-
-        def split(target, carry):
-            base = target * (CORES * PIECE)
-            for r in range(PIECE):
-                for ref, side in ((keep_ref, core), (send_ref, 1 - core)):
-                    first = base + side * PIECE + r
-                    ref[target, pl.ds(r * GROUPS, GROUPS), :] = acc_ref[
-                        pl.ds(first, GROUPS, stride=ROWS_G), :
-                    ].astype(ref.dtype)
-            return carry
-
-        lax.fori_loop(0, ZS * YS, split, 0)
-
-
-def attend(positions, core, masks, queries, blocks):
+        for z in range(0, ZS, 2):
+            part = pl.ds(z * YS, 2 * YS)
+            lax.fori_loop(z * YS, (z + 2) * YS, split, 0, unroll=4)
+            copy = pltpu.make_async_copy(ref.at[part], hbm.at[part], out_sems.at[out * ZS + z])
+            copy.start()
+            copies.append(copy)
+    for copy in copies:
+        copy.wait()
+
+
+def attend(positions, core, masks, payload, blocks):
     piece = jax.ShapeDtypeStruct((ZS * YS, GROUPS * PIECE, DH), jnp.bfloat16)
-    whole = pl.BlockSpec((ZS * YS, GROUPS * PIECE, DH), lambda i, *_: (0, 0, 0))
-    flops = 4 * BLOCKS_HERE * CAND * BLK * DH
+    smem, hbm = pl.BlockSpec(memory_space=pltpu.SMEM), pl.BlockSpec(memory_space=pltpu.HBM)
     return pl.pallas_call(
         attend_kernel,
         out_shape=(piece, piece),
-        grid_spec=pltpu.PrefetchScalarGridSpec(
-            num_scalar_prefetch=3,
-            grid=(BLOCKS_HERE // KV_STEP,),
-            in_specs=[
-                pl.BlockSpec((REQUESTS * CAND, DH), lambda i, *_: (0, 0)),
-                pl.BlockSpec((KV_STEP, BLK, SLAB), lambda i, *_: (i, 0, 0)),
-            ],
-            out_specs=(whole, whole),
-            scratch_shapes=[pltpu.VMEM((REQUESTS * CAND, DH), jnp.float32)],
+        in_specs=[smem, smem, smem, hbm, hbm],
+        out_specs=(hbm, hbm),
+        scratch_shapes=[
+            pltpu.VMEM((GROUPS, ROWS_G, DH), payload.dtype),
+            pltpu.VMEM(blocks.shape, blocks.dtype),
+            pltpu.VMEM((REQUESTS * CAND, DH), jnp.float32),
+            pltpu.VMEM(piece.shape, piece.dtype),
+            pltpu.VMEM(piece.shape, piece.dtype),
+            pltpu.SemaphoreType.DMA((GROUPS,)),
+            pltpu.SemaphoreType.DMA((BLOCKS_HERE // KV_STEP,)),
+            pltpu.SemaphoreType.DMA((2 * ZS,)),
+        ],
+        compiler_params=pltpu.CompilerParams(vmem_limit_bytes=60 << 20),
+        cost_estimate=pl.CostEstimate(
+            flops=4 * BLOCKS_HERE * CAND * BLK * DH,
+            bytes_accessed=10 << 20,
+            transcendentals=BLOCKS_HERE * CAND * BLK,
         ),
-        compiler_params=pltpu.CompilerParams(
-            vmem_limit_bytes=40 << 20, dimension_semantics=("arbitrary",)
-        ),
-        cost_estimate=pl.CostEstimate(
-            flops=flops, bytes_accessed=10 << 20, transcendentals=BLOCKS_HERE * CAND * BLK
-        ),
-    )(positions, core, masks, queries, blocks)
+    )(positions, core, masks, payload, blocks)
 
 
 def finish_kernel(back_ref, gain_ref, gate_ref, token_ref, w_ref, out_ref):
@@ -216,11 +257,13 @@
     yc = lax.axis_index(("y", "core"))
     packed = pack(me, owner_ids, slot_ids, kv_cache)
     arrived = lax.all_to_all(packed, ("cuts", "z"), split_axis=0, concat_axis=0, tiled=True)
-    query_all = lax.all_gather(queries.reshape(ROWS_G, DH), ("y", "core"), axis=0, tiled=True)
-    w_all = lax.all_gather(w_out, ("z", "y", "core"), axis=0, tiled=True)
+    payload = jnp.concatenate([queries.reshape(ROWS_G, DH), w_out.reshape(W_ROWS, DH)], axis=0)
+    payload = lax.all_gather(payload, ("y", "core"), axis=0, tiled=True).reshape(GROUPS, PAYLOAD, DH)
+    w_head = payload[:, ROWS_G:].reshape(DH, H * DH)
+    w_all = lax.all_gather(w_head, "z", axis=0, tiled=True)
     positions, masks = describe(cut, yc, hist_blocks, ranker_list, owner_ids, block_mask)
     keep, send = attend(
-        positions, core.reshape(1), masks, query_all, arrived.reshape(BLOCKS_HERE, BLK, SLAB)
+        positions, core.reshape(1), masks, payload, arrived.reshape(BLOCKS_HERE, BLK, SLAB)
     )
     other = lax.ppermute(send, "core", [(0, 1), (1, 0)])
     both = (keep.astype(jnp.float32) + other.astype(jnp.float32)).astype(jnp.bfloat16)

time: 265 us -> 224 us (0.85); the launches traced: 265 us -> 221 us
  waiting for transfers between devices: 182 us -> 144 us
  local copies, waits for them, and re-layouts: 14.9 us -> 9.34 us
    all_gather x2, waiting for transfers between devices: 133 us -> 98.4 us  [the longest x1 57.6 us: local(): w_all = lax.all_gather(w_head, 'z', axis=0, tiled=True)]
    unnamed x18 -> x14, local copies, waits for them, and re-layouts: 9.56 us -> 1.61 us
    pallas_call x1, Pallas kernels: 16.7 us -> 13 us  [attend(): pl.pallas_call(attend_kernel, out_shape=(piece, piece), in_specs=[smem, s...]
    pallas_call x1, Pallas kernels: 2.51 us -> 5.25 us  [pack(): pl.pallas_call(pack_kernel, out_shape=jax.ShapeDtypeStruct((SOURCES, OWN,...]
  transfers between devices with their start and end apart: 5 -> 5, of which waited for: 4 -> 4; matrix products, arithmetic and copies ran while one was open for 3% -> 6% of each run, Pallas kernels for 0% -> 0%
where the time goes in v2:
time: 224 us; the launch traced here: 221 us
  waiting for transfers between devices  144 us (64%)
  starting transfers between devices  29.3 us (13%)
  Pallas kernels  19.7 us (9%)
  between operations  13.6 us (6%)
  local copies, waits for them, and re-layouts  9.34 us (4%)
  other arithmetic  4.83 us (2%)
    all_gather x1, waiting for transfers between devices, local(): w_all = lax.all_gather(w_head, 'z', axis=0, tiled=True)  57.6 us
    all_to_all x1, waiting for transfers between devices, local(): lax.all_to_all(packed, ('cuts', 'z'), split_axis=0, concat_axis=0, tiled=...  44.1 us
    all_gather x1, waiting for transfers between devices, local(): lax.all_gather(payload, ('y', 'core'), axis=0, tiled=True)  40.7 us
    all_to_all x1, starting transfers between devices, local(): lax.all_to_all(packed, ('cuts', 'z'), split_axis=0, concat_axis=0, tiled=...  14 us
    pallas_call x1, Pallas kernels, attend(): pl.pallas_call(attend_kernel, out_shape=(piece, piece), in_specs=[smem, s...  13 us
    all_to_all x1, starting transfers between devices, local(): lax.all_to_all(both, ('z', 'y'), split_axis=0, concat_axis=0, tiled=True)  7.96 us
    ppermute x1, starting transfers between devices, local(): other = lax.ppermute(send, 'core', [(0, 1), (1, 0)])  7.28 us
    pallas_call x1, Pallas kernels, pack(): pl.pallas_call(pack_kernel, out_shape=jax.ShapeDtypeStruct((SOURCES, OWN,...  5.25 us
  transfers between devices with their start and end apart: 5, of which 4 were waited for; matrix products, arithmetic and copies ran while one was open for 6% of the time, Pallas kernels for 0%

profile of v2, /device:TPU:1, one launch (start us, length us, event | category | flops | bytes accessed | tf_op | source)
XLA Modules:
  0.0 220.6 jit_solution(13572850738418117121)
XLA Ops:
  6.5 0.0 copy-start
  6.5 5.3 %shard_map.109 = bf16[32,2,128,256]{3,2,1,0:T(8,128)(2,1)} custom-call(s32[1]{0:T(128)} %bitcast.10.self_ref, s32[4,32,64]{2,1,0:T(8,128)} %bitcast.40, s32[4,32,64]{2,1,0:T(8,128)} %bitcast.41, bf16[8,128,2048]{2,1,0:T(8,128)(2,1)} %kv_ref.1), custom_call_target="tpu_custom_call" | custom-call | tf_op jit(solution)/shard_map/pallas_call | solution.py:73
  11.8 0.0 copy-start.6
  11.8 0.0 copy-start.5
  11.8 14.0 %all-to-all-start = ((bf16[32,2,128,256]{3,2,1,0:T(8,128)(2,1)}), bf16[32,2,128,256]{3,2,1,0:T(8,128)(2,1)}, u32[]{:S(2)}, u32[]{:S(2)}) async-start(bf16[32,2,128,256]{3,2,1,0:T(8,128)(2,1)} %shard_map.109), calls=%async_computation | async-start | bytes 8388608 | tf_op jit(solution)/shard_map/all_to_all | solution.py:259
  25.8 0.0 all-gather.3.cloned.1.call-start
  25.9 0.0 copy-done.6
  25.9 0.0 copy-done.5
  25.9 0.7 pad_maximum_fusion
  26.6 0.0 all-gather.3.cloned.1.call-update
  26.6 0.0 all-gather.5.cloned.1.call-start
  26.7 0.7 constant_dynamic-slice_fusion.2
  27.4 0.1 copy.19
  27.5 0.1 eq.36
  27.6 0.2 fusion
  27.8 0.1 copy.20
  27.9 0.1 reshape.220
  28.0 0.1 reshape.218
  28.1 0.0 copy-done
  28.2 0.9 copy.21
  29.1 0.7 fusion.6
  29.8 0.8 gather_fusion.1
  30.6 0.9 gather_fusion
  31.5 0.1 convert_multiply_fusion
  31.6 0.7 mul.49.mask_ref
  32.3 0.7 fusion.5
  33.0 0.8 select_reduce_fusion.pos_ref
  33.8 40.7 %all-gather.3.cloned.1.call-done = bf16[13312,128]{1,0:T(8,128)(2,1)} async-done(((bf16[832,128]{1,0:T(8,128)(2,1)}), bf16[13312,128]{1,0:T(8,128)(2,1)}) %all-gather.3.cloned.1.call-update) | async-done | bytes 3407888 | tf_op jit(solution)/shard_map/all_gather | solution.py:261
  74.5 44.1 %all-to-all-done = bf16[32,2,128,256]{3,2,1,0:T(8,128)(2,1)} async-done(((bf16[32,2,128,256]{3,2,1,0:T(8,128)(2,1)}), bf16[32,2,128,256]{3,2,1,0:T(8,128)(2,1)}, u32[]{:S(2)}, u32[]{:S(2)}) %all-to-all-start) | async-done | bytes 4194336 | tf_op jit(solution)/shard_map/all_to_all | solution.py:259
  118.6 13.0 %shard_map.110 = (bf16[64,96,128]{2,1,0:T(8,128)(2,1)}, bf16[64,96,128]{2,1,0:T(8,128)(2,1)}) custom-call(s32[64]{0:T(128)} %select_reduce_fusion.pos_ref, s32[1]{0:T(128)} %bitcast.3.core_ref, f32[384]{0:T(512)} %mul.49.mask_ref, bf16[16,832,128]{2,1,0:T(8,128)(2,1)} %bitcast.36, bf16[64,128,256]{2,1,0:T(8,128)(2,1)} %bitcast.13.kv_hbm), custom_call_target="tpu_custom_call" | custom-call | flops 805306368 | bytes 10485760 | tf_op jit(solution)/shard_map/pallas_call | solution.py:170
  131.6 7.3 %collective-permute-start = (bf16[64,96,128]{2,1,0:T(8,128)(2,1)}, bf16[64,96,128]{2,1,0:T(8,128)(2,1)S(1)}, u32[]{:S(2)}, u32[]{:S(2)}) collective-permute-start(bf16[64,96,128]{2,1,0:T(8,128)(2,1)} %get-tuple-element.8), channel_id=1, source_target_pairs={{0,1},{1,0},{2,3},{3,2},{4,5},{5,4},{6,7},{7,6},{8,9},{9,8},{10,11... | collective-permute-start | bytes 4718600 | tf_op jit(solution)/shard_map/ppermute | solution.py:268
  138.8 1.0 slice.8
  139.8 0.8 reshape.231
  140.7 0.0 all-gather.5.cloned.1.call-update
  140.7 1.4 collective-permute-done
  142.1 3.0 %add_convert_fusion = bf16[64,96,128]{2,1,0:T(8,128)(2,1)} fusion(bf16[64,96,128]{2,1,0:T(8,128)(2,1)S(1)} %collective-permute-done, bf16[64,96,128]{2,1,0:T(8,128)(2,1)} %get-tuple-element.7), kind=kLoop, calls=%fused_computation.2 | loop fusion | flops 3145728 | bytes 4718592 | tf_op jit(solution)/shard_map/convert_element_type | solution.py:269
  145.0 0.0 copy-start.2
  145.0 0.0 copy-start.3
  145.1 0.0 copy-start.4
  145.1 8.0 %all-to-all-start.1 = ((bf16[64,96,128]{2,1,0:T(8,128)(2,1)}), bf16[64,96,128]{2,1,0:T(8,128)(2,1)S(1)}, u32[]{:S(2)}, u32[]{:S(2)}) async-start(bf16[64,96,128]{2,1,0:T(8,128)(2,1)} %add_convert_fusion), calls=%async_computation.1 | async-start | bytes 3145728 | tf_op jit(solution)/shard_map/all_to_all | solution.py:270
  153.0 57.6 %all-gather.5.cloned.1.call-done.w_ref = bf16[1024,1024]{1,0:T(8,128)(2,1)} async-done(((bf16[128,1024]{1,0:T(8,128)(2,1)}), bf16[1024,1024]{1,0:T(8,128)(2,1)}) %all-gather.5.cloned.1.call-update) | async-done | bytes 2097168 | tf_op jit(solution)/shard_map/all_gather | solution.py:263
  210.7 0.0 all-to-all-done.1.back_ref
  210.7 0.0 copy-done.2
  210.7 0.0 copy-done.3
  210.7 0.0 copy-done.4
  210.7 0.0 copy-start.1
  210.7 1.6 copy-done.1
  212.3 1.5 shard_map.111
  (8 shorter events, 0.1 us)
Async XLA Ops:
  6.5 21.6 %copy-start = (s32[4,64,6,32]{1,3,2,0:T(8,128)S(1)}, s32[4,64,6,32]{1,3,2,0:T(8,128)}, u32[]{:S(2)}) copy-start(s32[4,64,6,32]{1,3,2,0:T(8,128)} %param.21) | copy-start | bytes 589828
  11.8 14.1 %copy-start.6 = (bf16[8,1024]{1,0:T(8,128)(2,1)S(1)}, bf16[8,1024]{1,0:T(8,128)(2,1)}, u32[]{:S(2)}) copy-start(bf16[8,1024]{1,0:T(8,128)(2,1)} %param.15) | copy-start | bytes 49156
  11.8 14.1 %copy-start.5 = (bf16[1,1,768,128]{3,2,1,0:T(8,128)(2,1)S(1)}, bf16[1,1,768,128]{3,2,1,0:T(8,128)(2,1)}, u32[]{:S(2)}) copy-start(bf16[1,1,768,128]{3,2,1,0:T(8,128)(2,1)} %param.12) | copy-start | bytes 589828
  11.8 106.8 %all-to-all-start = ((bf16[32,2,128,256]{3,2,1,0:T(8,128)(2,1)}), bf16[32,2,128,256]{3,2,1,0:T(8,128)(2,1)}, u32[]{:S(2)}, u32[]{:S(2)}) async-start(bf16[32,2,128,256]{3,2,1,0:T(8,128)(2,1)} %shard_map.109), calls=%async_computation | async-start | bytes 8388608 | tf_op jit(solution)/shard_map/all_to_all | solution.py:259
  25.8 48.7 %all-gather.3.cloned.1.call-start = ((), (), s32[]{:S(2)}) async-start(), calls=%async_computation.2 | async-start | bytes 3620864 | tf_op jit(solution)/shard_map/all_gather | solution.py:261
  26.6 184.0 %all-gather.5.cloned.1.call-start = ((), (), s32[]{:S(2)}) async-start(), calls=%async_computation.3 | async-start | bytes 2359296 | tf_op jit(solution)/shard_map/all_gather | solution.py:263
  131.6 10.5 %collective-permute-start = (bf16[64,96,128]{2,1,0:T(8,128)(2,1)}, bf16[64,96,128]{2,1,0:T(8,128)(2,1)S(1)}, u32[]{:S(2)}, u32[]{:S(2)}) collective-permute-start(bf16[64,96,128]{2,1,0:T(8,128)(2,1)} %get-tuple-element.8), channel_id=1, source_target_pairs={{0,1},{1,0},{2,3},{3,2},{4,5},{5,4},{6,7},{7,6},{8,9},{9,8},{10,11... | collective-permute-start | bytes 4718600 | tf_op jit(solution)/shard_map/ppermute | solution.py:268
  145.0 65.6 %copy-start.2 = (bf16[1,16,6,1024]{3,1,2,0:T(8,128)(2,1)S(1)}, bf16[1,16,6,1024]{3,1,2,0:T(8,128)(2,1)}, u32[]{:S(2)}) copy-start(bf16[1,16,6,1024]{3,1,2,0:T(8,128)(2,1)} %param.13) | copy-start | bytes 589828
  145.0 65.6 %copy-start.3 = (bf16[1,16,6,1024]{3,1,2,0:T(8,128)(2,1)S(1)}, bf16[1,16,6,1024]{3,1,2,0:T(8,128)(2,1)}, u32[]{:S(2)}) copy-start(bf16[1,16,6,1024]{3,1,2,0:T(8,128)(2,1)} %param.14) | copy-start | bytes 589828
  145.1 65.6 %copy-start.4 = (f32[1024]{0:T(1024)S(1)}, f32[1024]{0:T(1024)}, u32[]{:S(2)}) copy-start(f32[1024]{0:T(1024)} %param.16) | copy-start | bytes 12292
  145.1 65.6 %all-to-all-start.1 = ((bf16[64,96,128]{2,1,0:T(8,128)(2,1)}), bf16[64,96,128]{2,1,0:T(8,128)(2,1)S(1)}, u32[]{:S(2)}, u32[]{:S(2)}) async-start(bf16[64,96,128]{2,1,0:T(8,128)(2,1)} %add_convert_fusion), calls=%async_computation.1 | async-start | bytes 3145728 | tf_op jit(solution)/shard_map/all_to_all | solution.py:270
  210.7 1.6 copy-start.1
Sparse Core Ops, SparseCore 0:
  28.8 45.6 all-gather.2
  140.8 69.7 all-gather.4

commit v3 on v2

--- a/solution.py
+++ b/solution.py
@@ -24,8 +24,6 @@
 BLOCKS_HERE = SOURCES * OWN
 KV_STEP = 8
 EPS = 1e-05
-W_ROWS = 64
-PAYLOAD = ROWS_G + W_ROWS
 
 
 def pack_kernel(self_ref, owner_hbm, slot_hbm, kv_ref, out_ref, owner_ref, slot_ref, held, sems, in_sems, out_sems):
@@ -257,16 +255,16 @@
     yc = lax.axis_index(("y", "core"))
     packed = pack(me, owner_ids, slot_ids, kv_cache)
     arrived = lax.all_to_all(packed, ("cuts", "z"), split_axis=0, concat_axis=0, tiled=True)
-    payload = jnp.concatenate([queries.reshape(ROWS_G, DH), w_out.reshape(W_ROWS, DH)], axis=0)
-    payload = lax.all_gather(payload, ("y", "core"), axis=0, tiled=True).reshape(GROUPS, PAYLOAD, DH)
-    w_head = payload[:, ROWS_G:].reshape(DH, H * DH)
-    w_all = lax.all_gather(w_head, "z", axis=0, tiled=True)
+    payload = lax.all_gather(queries.reshape(ROWS_G, DH), ("y", "core"), axis=0, tiled=True)
+    payload = payload.reshape(GROUPS, ROWS_G, DH)
+    w_all = lax.all_gather(w_out, ("z", "y", "core"), axis=0, tiled=True)
     positions, masks = describe(cut, yc, hist_blocks, ranker_list, owner_ids, block_mask)
     keep, send = attend(
         positions, core.reshape(1), masks, payload, arrived.reshape(BLOCKS_HERE, BLK, SLAB)
     )
     other = lax.ppermute(send, "core", [(0, 1), (1, 0)])
     both = (keep.astype(jnp.float32) + other.astype(jnp.float32)).astype(jnp.bfloat16)
+    both, w_all = lax.optimization_barrier((both, w_all))
     back = lax.all_to_all(both, ("z", "y"), split_axis=0, concat_axis=0, tiled=True)
     width = H * DH
     gate_rows = gates.reshape(GROUPS, PIECE, width).transpose(1, 0, 2).reshape(-1, width)

time: 224 us -> 229 us (1.022)
  blocking collectives: 0 us -> 47.8 us
  waiting for transfers between devices: 144 us -> 116 us
  starting transfers between devices: 29.3 us -> 21.1 us
  local copies, waits for them, and re-layouts: 9.34 us -> 5.98 us
    all_to_all x0 -> x1, blocking collectives: none -> 47.8 us  [local(): lax.all_to_all(both, ('z', 'y'), split_axis=0, concat_axis=0, tiled=True)]
    all_gather x2, waiting for transfers between devices: 98.4 us -> 66.7 us  [the longest x1 39.7 us: local(): lax.all_gather(queries.reshape(ROWS_G, DH), ('y', 'core'), axis=0, tiled=...]
    all_to_all x1 -> x0, starting transfers between devices: 7.96 us -> none  [local(): lax.all_to_all(both, ('z', 'y'), split_axis=0, concat_axis=0, tiled=True)]
  transfers between devices with their start and end apart: 5 -> 4, of which waited for: 4 -> 4; matrix products, arithmetic and copies ran while one was open for 6% -> 4% of each run, Pallas kernels for 0% -> 6%
where the time goes in v3:
time: 229 us; the launch traced here: 227 us
  waiting for transfers between devices  116 us (51%)
  blocking collectives  47.8 us (21%)
  starting transfers between devices  21.1 us (9%)
  Pallas kernels  19.7 us (9%)
  between operations  13.5 us (6%)
  local copies, waits for them, and re-layouts  5.98 us (3%)
  other arithmetic  2.97 us (1%)
    all_to_all x1, blocking collectives, local(): lax.all_to_all(both, ('z', 'y'), split_axis=0, concat_axis=0, tiled=True)  47.8 us
    all_to_all x1, waiting for transfers between devices, local(): lax.all_to_all(packed, ('cuts', 'z'), split_axis=0, concat_axis=0, tiled=...  44.9 us
    all_gather x1, waiting for transfers between devices, local(): lax.all_gather(queries.reshape(ROWS_G, DH), ('y', 'core'), axis=0, tiled=...  39.7 us
    all_gather x1, waiting for transfers between devices, local(): w_all = lax.all_gather(w_out, ('z', 'y', 'core'), axis=0, tiled=True)  27 us
    all_to_all x1, starting transfers between devices, local(): lax.all_to_all(packed, ('cuts', 'z'), split_axis=0, concat_axis=0, tiled=...  13.9 us
    pallas_call x1, Pallas kernels, attend(): pl.pallas_call(attend_kernel, out_shape=(piece, piece), in_specs=[smem, s...  13 us
    ppermute x1, starting transfers between devices, local(): other = lax.ppermute(send, 'core', [(0, 1), (1, 0)])  7.17 us
    pallas_call x1, Pallas kernels, pack(): pl.pallas_call(pack_kernel, out_shape=jax.ShapeDtypeStruct((SOURCES, OWN,...  5.28 us
  transfers between devices with their start and end apart: 4, of which 4 were waited for; matrix products, arithmetic and copies ran while one was open for 4% of the time, Pallas kernels for 6%

profile of v3, /device:TPU:1, one launch (start us, length us, event | category | flops | bytes accessed | tf_op | source)
XLA Modules:
  0.0 227.4 jit_solution(13284629121803819228)
XLA Ops:
  6.5 0.0 copy-start
  6.5 5.3 %shard_map.109 = bf16[32,2,128,256]{3,2,1,0:T(8,128)(2,1)} custom-call(s32[1]{0:T(128)} %bitcast.9.self_ref, s32[4,32,64]{2,1,0:T(8,128)} %bitcast.37, s32[4,32,64]{2,1,0:T(8,128)} %bitcast.38, bf16[8,128,2048]{2,1,0:T(8,128)(2,1)} %kv_ref.1), custom_call_target="tpu_custom_call" | custom-call | tf_op jit(solution)/shard_map/pallas_call | solution.py:71
  11.8 13.9 %all-to-all-start = ((bf16[32,2,128,256]{3,2,1,0:T(8,128)(2,1)}), bf16[32,2,128,256]{3,2,1,0:T(8,128)(2,1)}, u32[]{:S(2)}, u32[]{:S(2)}) async-start(bf16[32,2,128,256]{3,2,1,0:T(8,128)(2,1)} %shard_map.109), calls=%async_computation | async-start | bytes 8388608 | tf_op jit(solution)/shard_map/all_to_all | solution.py:257
  25.7 0.0 all-gather.6.cloned.1.call-start
  25.7 0.7 all-gather.6.cloned.1.call-update
  26.4 0.0 all-gather.4.cloned.1.call-start
  26.5 0.7 all-gather.4.cloned.1.call-update
  27.2 0.7 constant_dynamic-slice_fusion.2
  27.9 0.1 copy.19
  28.0 0.1 eq.36
  28.1 0.2 fusion
  28.3 0.1 copy.20
  28.4 0.1 reshape.214
  28.5 0.1 reshape.212
  28.6 0.0 copy-done
  28.7 1.0 copy.21
  29.7 0.7 fusion.6
  30.4 0.8 gather_fusion.1
  31.2 0.9 gather_fusion
  32.1 0.1 convert_multiply_fusion
  32.1 0.7 mul.49.mask_ref
  32.9 0.7 fusion.5
  33.6 0.8 select_reduce_fusion.pos_ref
  34.3 39.7 %all-gather.6.cloned.1.call-done = bf16[1,1,12288,128]{3,2,1,0:T(8,128)(2,1)} async-done(((bf16[1,1,768,128]{3,2,1,0:T(8,128)(2,1)}), bf16[1,1,12288,128]{3,2,1,0:T(8,128)(2,1)}) %all-gather.6.cloned.1.call-update) | async-done | bytes 3145744 | tf_op jit(solution)/shard_map/all_gather | solution.py:258
  74.1 44.9 %all-to-all-done = bf16[32,2,128,256]{3,2,1,0:T(8,128)(2,1)} async-done(((bf16[32,2,128,256]{3,2,1,0:T(8,128)(2,1)}), bf16[32,2,128,256]{3,2,1,0:T(8,128)(2,1)}, u32[]{:S(2)}, u32[]{:S(2)}) %all-to-all-start) | async-done | bytes 4194336 | tf_op jit(solution)/shard_map/all_to_all | solution.py:257
  119.0 13.0 %shard_map.110 = (bf16[64,96,128]{2,1,0:T(8,128)(2,1)}, bf16[64,96,128]{2,1,0:T(8,128)(2,1)}) custom-call(s32[64]{0:T(128)} %select_reduce_fusion.pos_ref, s32[1]{0:T(128)} %bitcast.3.core_ref, f32[384]{0:T(512)} %mul.49.mask_ref, bf16[16,768,128]{2,1,0:T(8,128)(2,1)} %bitcast.35, bf16[64,128,256]{2,1,0:T(8,128)(2,1)} %bitcast.12.kv_hbm), custom_call_target="tpu_custom_call" | custom-call | flops 805306368 | bytes 10485760 | tf_op jit(solution)/shard_map/pallas_call | solution.py:168
  132.0 7.2 %collective-permute-start = (bf16[64,96,128]{2,1,0:T(8,128)(2,1)}, bf16[64,96,128]{2,1,0:T(8,128)(2,1)S(1)}, u32[]{:S(2)}, u32[]{:S(2)}) collective-permute-start(bf16[64,96,128]{2,1,0:T(8,128)(2,1)} %get-tuple-element.10), channel_id=1, source_target_pairs={{0,1},{1,0},{2,3},{3,2},{4,5},{5,4},{6,7},{7,6},{8,9},{9,8},{10,11... | collective-permute-start | bytes 4718600 | tf_op jit(solution)/shard_map/ppermute | solution.py:265
  139.1 3.2 %collective-permute-done = bf16[64,96,128]{2,1,0:T(8,128)(2,1)S(1)} collective-permute-done((bf16[64,96,128]{2,1,0:T(8,128)(2,1)}, bf16[64,96,128]{2,1,0:T(8,128)(2,1)S(1)}, u32[]{:S(2)}, u32[]{:S(2)}) %collective-permute-start) | collective-permute-done | bytes 1572896 | tf_op jit(solution)/shard_map/ppermute | solution.py:265
  142.4 1.8 add_convert_fusion
  144.2 0.0 copy-start.2
  144.2 0.0 copy-start.3
  144.2 0.0 copy-start.4
  144.2 27.0 %all-gather.4.cloned.1.call-done.w_ref = bf16[1024,1024]{1,0:T(8,128)(2,1)} async-done(((bf16[8,1024]{1,0:T(8,128)(2,1)}), bf16[1024,1024]{1,0:T(8,128)(2,1)}) %all-gather.4.cloned.1.call-update) | async-done | bytes 2097168 | tf_op jit(solution)/shard_map/all_gather | solution.py:260
  171.2 0.0 copy-start.1
  171.2 47.8 %all_to_all.10.back_ref = bf16[64,96,128]{2,1,0:T(8,128)(2,1)S(1)} all-to-all(bf16[64,96,128]{2,1,0:T(8,128)(2,1)S(1)} %add_convert_fusion), channel_id=1, replica_groups=mesh['cuts'=4,'z'=8,'y'=8,'core'=2] {'z','y'}, dimensions={0} | all-to-all | bytes 3145728 | tf_op jit(solution)/shard_map/all_to_all | solution.py:268
  219.0 0.0 copy-done.2
  219.1 0.0 copy-done.3
  219.1 0.0 copy-done.4
  219.1 0.0 copy-done.1
  219.1 1.5 shard_map.111
  (7 shorter events, 0.1 us)
Async XLA Ops:
  6.5 22.1 %copy-start = (s32[4,64,6,32]{1,3,2,0:T(8,128)S(1)}, s32[4,64,6,32]{1,3,2,0:T(8,128)}, u32[]{:S(2)}) copy-start(s32[4,64,6,32]{1,3,2,0:T(8,128)} %param.21) | copy-start | bytes 589828
  11.8 107.2 %all-to-all-start = ((bf16[32,2,128,256]{3,2,1,0:T(8,128)(2,1)}), bf16[32,2,128,256]{3,2,1,0:T(8,128)(2,1)}, u32[]{:S(2)}, u32[]{:S(2)}) async-start(bf16[32,2,128,256]{3,2,1,0:T(8,128)(2,1)} %shard_map.109), calls=%async_computation | async-start | bytes 8388608 | tf_op jit(solution)/shard_map/all_to_all | solution.py:257
  25.7 48.4 %all-gather.6.cloned.1.call-start = ((), (), s32[]{:S(2)}) async-start(), calls=%async_computation.3 | async-start | bytes 3342336 | tf_op jit(solution)/shard_map/all_gather | solution.py:258
  26.4 144.8 %all-gather.4.cloned.1.call-start = ((), (), s32[]{:S(2)}) async-start(), calls=%async_computation.2 | async-start | bytes 2113536 | tf_op jit(solution)/shard_map/all_gather | solution.py:260
  132.0 10.4 %collective-permute-start = (bf16[64,96,128]{2,1,0:T(8,128)(2,1)}, bf16[64,96,128]{2,1,0:T(8,128)(2,1)S(1)}, u32[]{:S(2)}, u32[]{:S(2)}) collective-permute-start(bf16[64,96,128]{2,1,0:T(8,128)(2,1)} %get-tuple-element.10), channel_id=1, source_target_pairs={{0,1},{1,0},{2,3},{3,2},{4,5},{5,4},{6,7},{7,6},{8,9},{9,8},{10,11... | collective-permute-start | bytes 4718600 | tf_op jit(solution)/shard_map/ppermute | solution.py:265
  144.2 74.9 %copy-start.2 = (bf16[1,16,6,1024]{3,1,2,0:T(8,128)(2,1)S(1)}, bf16[1,16,6,1024]{3,1,2,0:T(8,128)(2,1)}, u32[]{:S(2)}) copy-start(bf16[1,16,6,1024]{3,1,2,0:T(8,128)(2,1)} %param.13) | copy-start | bytes 589828
  144.2 74.9 %copy-start.3 = (bf16[1,16,6,1024]{3,1,2,0:T(8,128)(2,1)S(1)}, bf16[1,16,6,1024]{3,1,2,0:T(8,128)(2,1)}, u32[]{:S(2)}) copy-start(bf16[1,16,6,1024]{3,1,2,0:T(8,128)(2,1)} %param.14) | copy-start | bytes 589828
  144.2 74.8 %copy-start.4 = (f32[1024]{0:T(1024)S(1)}, f32[1024]{0:T(1024)}, u32[]{:S(2)}) copy-start(f32[1024]{0:T(1024)} %param.16) | copy-start | bytes 12292
  171.2 47.9 %copy-start.1 = (bf16[1024,1024]{1,0:T(8,128)(2,1)S(1)}, bf16[1024,1024]{1,0:T(8,128)(2,1)}, u32[]{:S(2)}) copy-start(bf16[1024,1024]{1,0:T(8,128)(2,1)} %all-gather.4.cloned.1.call-done.w_ref) | copy-start | bytes 6291460
Sparse Core Ops, SparseCore 0:
  28.6 45.3 all-gather.5
  77.2 93.9 all-gather.3

commit v4 on v2

--- a/solution.py
+++ b/solution.py
@@ -267,6 +267,7 @@
     )
     other = lax.ppermute(send, "core", [(0, 1), (1, 0)])
     both = (keep.astype(jnp.float32) + other.astype(jnp.float32)).astype(jnp.bfloat16)
+    both, w_all = lax.optimization_barrier((both, w_all))
     back = lax.all_to_all(both, ("z", "y"), split_axis=0, concat_axis=0, tiled=True)
     width = H * DH
     gate_rows = gates.reshape(GROUPS, PIECE, width).transpose(1, 0, 2).reshape(-1, width)

time: 224 us -> 213 us (0.951)
  waiting for transfers between devices: 144 us -> 91 us
  blocking collectives: 0 us -> 50.3 us
  starting transfers between devices: 29.3 us -> 24.2 us
    all_gather x1, waiting for transfers between devices: 57.6 us -> 0.02 us  [local(): w_all = lax.all_gather(w_head, 'z', axis=0, tiled=True)]
    all_to_all x0 -> x1, blocking collectives: none -> 50.3 us  [local(): lax.all_to_all(both, ('z', 'y'), split_axis=0, concat_axis=0, tiled=True)]
    all_to_all x1 -> x0, starting transfers between devices: 7.96 us -> none  [local(): lax.all_to_all(both, ('z', 'y'), split_axis=0, concat_axis=0, tiled=True)]
    all_gather x1, waiting for transfers between devices: 40.7 us -> 47 us  [local(): lax.all_gather(payload, ('y', 'core'), axis=0, tiled=True)]
    all_to_all x1, waiting for transfers between devices: 44.1 us -> 40.8 us  [local(): lax.all_to_all(packed, ('cuts', 'z'), split_axis=0, concat_axis=0, tiled=...]
    ppermute x1, starting transfers between devices: 7.28 us -> 10.1 us  [local(): other = lax.ppermute(send, 'core', [(0, 1), (1, 0)])]
  transfers between devices with their start and end apart: 5 -> 4, of which waited for: 4 -> 3; matrix products, arithmetic and copies ran while one was open for 6% -> 5% of each run, Pallas kernels for 0% -> 6%
where the time goes in v4:
time: 213 us; the launch traced here: 210 us
  waiting for transfers between devices  91 us (43%)
  blocking collectives  50.3 us (24%)
  starting transfers between devices  24.2 us (11%)
  Pallas kernels  19.7 us (9%)
  between operations  13.6 us (6%)
  local copies, waits for them, and re-layouts  7.82 us (4%)
  other arithmetic  3.58 us (2%)
    all_to_all x1, blocking collectives, local(): lax.all_to_all(both, ('z', 'y'), split_axis=0, concat_axis=0, tiled=True)  50.3 us
    all_gather x1, waiting for transfers between devices, local(): lax.all_gather(payload, ('y', 'core'), axis=0, tiled=True)  47 us
    all_to_all x1, waiting for transfers between devices, local(): lax.all_to_all(packed, ('cuts', 'z'), split_axis=0, concat_axis=0, tiled=...  40.8 us
    all_to_all x1, starting transfers between devices, local(): lax.all_to_all(packed, ('cuts', 'z'), split_axis=0, concat_axis=0, tiled=...  14 us
    pallas_call x1, Pallas kernels, attend(): pl.pallas_call(attend_kernel, out_shape=(piece, piece), in_specs=[smem, s...  13 us
    ppermute x1, starting transfers between devices, local(): other = lax.ppermute(send, 'core', [(0, 1), (1, 0)])  10.1 us
    pallas_call x1, Pallas kernels, pack(): pl.pallas_call(pack_kernel, out_shape=jax.ShapeDtypeStruct((SOURCES, OWN,...  5.24 us
  transfers between devices with their start and end apart: 4, of which 3 were waited for; matrix products, arithmetic and copies ran while one was open for 5% of the time, Pallas kernels for 6%

profile of v4, /device:TPU:1, one launch (start us, length us, event | category | flops | bytes accessed | tf_op | source)
XLA Modules:
  0.0 210.2 jit_solution(8918273266862716366)
XLA Ops:
  6.5 0.0 copy-start
  6.5 5.2 %shard_map.109 = bf16[32,2,128,256]{3,2,1,0:T(8,128)(2,1)} custom-call(s32[1]{0:T(128)} %bitcast.10.self_ref, s32[4,32,64]{2,1,0:T(8,128)} %bitcast.40, s32[4,32,64]{2,1,0:T(8,128)} %bitcast.41, bf16[8,128,2048]{2,1,0:T(8,128)(2,1)} %kv_ref.1), custom_call_target="tpu_custom_call" | custom-call | tf_op jit(solution)/shard_map/pallas_call | solution.py:73
  11.8 0.0 copy-start.6
  11.8 0.0 copy-start.5
  11.8 14.0 %all-to-all-start = ((bf16[32,2,128,256]{3,2,1,0:T(8,128)(2,1)}), bf16[32,2,128,256]{3,2,1,0:T(8,128)(2,1)}, u32[]{:S(2)}, u32[]{:S(2)}) async-start(bf16[32,2,128,256]{3,2,1,0:T(8,128)(2,1)} %shard_map.109), calls=%async_computation | async-start | bytes 8388608 | tf_op jit(solution)/shard_map/all_to_all | solution.py:259
  25.8 0.0 all-gather.3.cloned.1.call-start
  25.9 0.0 copy-done.6
  25.9 0.0 copy-done.5
  25.9 0.7 pad_maximum_fusion
  26.6 0.0 all-gather.3.cloned.1.call-update
  26.6 0.0 all-gather.5.cloned.1.call-start
  26.7 0.7 constant_dynamic-slice_fusion.2
  27.4 0.1 copy.19
  27.5 0.1 eq.36
  27.5 47.0 %all-gather.3.cloned.1.call-done = bf16[13312,128]{1,0:T(8,128)(2,1)} async-done(((bf16[832,128]{1,0:T(8,128)(2,1)}), bf16[13312,128]{1,0:T(8,128)(2,1)}) %all-gather.3.cloned.1.call-update) | async-done | bytes 3407888 | tf_op jit(solution)/shard_map/all_gather | solution.py:261
  74.5 1.0 slice.8
  75.5 0.8 reshape.226
  76.3 0.0 all-gather.5.cloned.1.call-update
  76.4 0.2 fusion
  76.6 0.1 copy.20
  76.7 0.1 reshape.220
  76.8 0.1 reshape.218
  76.9 0.0 copy-done
  76.9 1.0 copy.21
  77.9 0.7 fusion.6
  78.7 0.8 gather_fusion.1
  79.4 0.9 gather_fusion
  80.3 0.1 convert_multiply_fusion
  80.4 0.7 mul.49.mask_ref
  81.1 0.7 fusion.5
  81.8 0.7 select_reduce_fusion.pos_ref
  82.5 40.8 %all-to-all-done = bf16[32,2,128,256]{3,2,1,0:T(8,128)(2,1)} async-done(((bf16[32,2,128,256]{3,2,1,0:T(8,128)(2,1)}), bf16[32,2,128,256]{3,2,1,0:T(8,128)(2,1)}, u32[]{:S(2)}, u32[]{:S(2)}) %all-to-all-start) | async-done | bytes 4194336 | tf_op jit(solution)/shard_map/all_to_all | solution.py:259
  123.3 13.0 %shard_map.110 = (bf16[64,96,128]{2,1,0:T(8,128)(2,1)}, bf16[64,96,128]{2,1,0:T(8,128)(2,1)}) custom-call(s32[64]{0:T(128)} %select_reduce_fusion.pos_ref, s32[1]{0:T(128)} %bitcast.3.core_ref, f32[384]{0:T(512)} %mul.49.mask_ref, bf16[16,832,128]{2,1,0:T(8,128)(2,1)} %bitcast.37, bf16[64,128,256]{2,1,0:T(8,128)(2,1)} %bitcast.13.kv_hbm), custom_call_target="tpu_custom_call" | custom-call | flops 805306368 | bytes 10485760 | tf_op jit(solution)/shard_map/pallas_call | solution.py:170
  136.3 10.1 %collective-permute-start = (bf16[64,96,128]{2,1,0:T(8,128)(2,1)}, bf16[64,96,128]{2,1,0:T(8,128)(2,1)S(1)}, u32[]{:S(2)}, u32[]{:S(2)}) collective-permute-start(bf16[64,96,128]{2,1,0:T(8,128)(2,1)} %get-tuple-element.10), channel_id=1, source_target_pairs={{0,1},{1,0},{2,3},{3,2},{4,5},{5,4},{6,7},{7,6},{8,9},{9,8},{10,11... | collective-permute-start | bytes 4718600 | tf_op jit(solution)/shard_map/ppermute | solution.py:268
  146.4 3.2 %collective-permute-done = bf16[64,96,128]{2,1,0:T(8,128)(2,1)S(1)} collective-permute-done((bf16[64,96,128]{2,1,0:T(8,128)(2,1)}, bf16[64,96,128]{2,1,0:T(8,128)(2,1)S(1)}, u32[]{:S(2)}, u32[]{:S(2)}) %collective-permute-start) | collective-permute-done | bytes 1572896 | tf_op jit(solution)/shard_map/ppermute | solution.py:268
  149.7 1.8 add_convert_fusion
  151.5 0.0 copy-start.2
  151.5 0.0 copy-start.3
  151.5 0.0 copy-start.4
  151.5 0.0 all-gather.5.cloned.1.call-done.w_ref
  151.6 0.0 copy-start.1
  151.6 50.3 %all_to_all.10.back_ref = bf16[64,96,128]{2,1,0:T(8,128)(2,1)S(1)} all-to-all(bf16[64,96,128]{2,1,0:T(8,128)(2,1)S(1)} %add_convert_fusion), channel_id=1, replica_groups=mesh['cuts'=4,'z'=8,'y'=8,'core'=2] {'z','y'}, dimensions={0} | all-to-all | bytes 3145728 | tf_op jit(solution)/shard_map/all_to_all | solution.py:271
  201.9 0.0 copy-done.2
  201.9 0.0 copy-done.3
  201.9 0.0 copy-done.4
  201.9 0.0 copy-done.1
  201.9 1.5 shard_map.111
  (8 shorter events, 0.1 us)
Async XLA Ops:
  6.5 70.4 %copy-start = (s32[4,64,6,32]{1,3,2,0:T(8,128)S(1)}, s32[4,64,6,32]{1,3,2,0:T(8,128)}, u32[]{:S(2)}) copy-start(s32[4,64,6,32]{1,3,2,0:T(8,128)} %param.21) | copy-start | bytes 589828
  11.8 14.1 %copy-start.6 = (bf16[8,1024]{1,0:T(8,128)(2,1)S(1)}, bf16[8,1024]{1,0:T(8,128)(2,1)}, u32[]{:S(2)}) copy-start(bf16[8,1024]{1,0:T(8,128)(2,1)} %param.15) | copy-start | bytes 49156
  11.8 14.1 %copy-start.5 = (bf16[1,1,768,128]{3,2,1,0:T(8,128)(2,1)S(1)}, bf16[1,1,768,128]{3,2,1,0:T(8,128)(2,1)}, u32[]{:S(2)}) copy-start(bf16[1,1,768,128]{3,2,1,0:T(8,128)(2,1)} %param.12) | copy-start | bytes 589828
  11.8 111.5 %all-to-all-start = ((bf16[32,2,128,256]{3,2,1,0:T(8,128)(2,1)}), bf16[32,2,128,256]{3,2,1,0:T(8,128)(2,1)}, u32[]{:S(2)}, u32[]{:S(2)}) async-start(bf16[32,2,128,256]{3,2,1,0:T(8,128)(2,1)} %shard_map.109), calls=%async_computation | async-start | bytes 8388608 | tf_op jit(solution)/shard_map/all_to_all | solution.py:259
  25.8 48.7 %all-gather.3.cloned.1.call-start = ((), (), s32[]{:S(2)}) async-start(), calls=%async_computation.2 | async-start | bytes 3620864 | tf_op jit(solution)/shard_map/all_gather | solution.py:261
  26.6 124.9 %all-gather.5.cloned.1.call-start = ((), (), s32[]{:S(2)}) async-start(), calls=%async_computation.3 | async-start | bytes 2359296 | tf_op jit(solution)/shard_map/all_gather | solution.py:263
  136.3 13.3 %collective-permute-start = (bf16[64,96,128]{2,1,0:T(8,128)(2,1)}, bf16[64,96,128]{2,1,0:T(8,128)(2,1)S(1)}, u32[]{:S(2)}, u32[]{:S(2)}) collective-permute-start(bf16[64,96,128]{2,1,0:T(8,128)(2,1)} %get-tuple-element.10), channel_id=1, source_target_pairs={{0,1},{1,0},{2,3},{3,2},{4,5},{5,4},{6,7},{7,6},{8,9},{9,8},{10,11... | collective-permute-start | bytes 4718600 | tf_op jit(solution)/shard_map/ppermute | solution.py:268
  151.5 50.4 %copy-start.2 = (bf16[1,16,6,1024]{3,1,2,0:T(8,128)(2,1)S(1)}, bf16[1,16,6,1024]{3,1,2,0:T(8,128)(2,1)}, u32[]{:S(2)}) copy-start(bf16[1,16,6,1024]{3,1,2,0:T(8,128)(2,1)} %param.13) | copy-start | bytes 589828
  151.5 50.4 %copy-start.3 = (bf16[1,16,6,1024]{3,1,2,0:T(8,128)(2,1)S(1)}, bf16[1,16,6,1024]{3,1,2,0:T(8,128)(2,1)}, u32[]{:S(2)}) copy-start(bf16[1,16,6,1024]{3,1,2,0:T(8,128)(2,1)} %param.14) | copy-start | bytes 589828
  151.5 50.4 %copy-start.4 = (f32[1024]{0:T(1024)S(1)}, f32[1024]{0:T(1024)}, u32[]{:S(2)}) copy-start(f32[1024]{0:T(1024)} %param.16) | copy-start | bytes 12292
  151.6 50.3 %copy-start.1 = (bf16[1024,1024]{1,0:T(8,128)(2,1)S(1)}, bf16[1024,1024]{1,0:T(8,128)(2,1)}, u32[]{:S(2)}) copy-start(bf16[1024,1024]{1,0:T(8,128)(2,1)} %all-gather.5.cloned.1.call-done.w_ref) | copy-start | bytes 6291460
Sparse Core Ops, SparseCore 0:
  28.8 45.6 all-gather.2
  76.6 65.1 all-gather.4

commit v5 on v4

--- a/solution.py
+++ b/solution.py
@@ -259,8 +259,8 @@
     arrived = lax.all_to_all(packed, ("cuts", "z"), split_axis=0, concat_axis=0, tiled=True)
     payload = jnp.concatenate([queries.reshape(ROWS_G, DH), w_out.reshape(W_ROWS, DH)], axis=0)
     payload = lax.all_gather(payload, ("y", "core"), axis=0, tiled=True).reshape(GROUPS, PAYLOAD, DH)
-    w_head = payload[:, ROWS_G:].reshape(DH, H * DH)
-    w_all = lax.all_gather(w_head, "z", axis=0, tiled=True)
+    w_head = lax.dynamic_slice_in_dim(payload[:, ROWS_G:], cut * (GROUPS // CUTS), GROUPS // CUTS)
+    w_all = lax.all_gather(w_head.reshape(DH // CUTS, H * DH), ("z", "cuts"), axis=0, tiled=True)
     positions, masks = describe(cut, yc, hist_blocks, ranker_list, owner_ids, block_mask)
     keep, send = attend(
         positions, core.reshape(1), masks, payload, arrived.reshape(BLOCKS_HERE, BLK, SLAB)

time: 213 us -> 217 us (1.019)
  the two profiles are of different devices: /device:TPU:1 before, /device:TPU:8 now
where the time goes in v5:
time: 217 us; the launch traced here: 216 us
  waiting for transfers between devices  108 us (50%)
  blocking collectives  46.8 us (22%)
  Pallas kernels  19.7 us (9%)
  starting transfers between devices  15.3 us (7%)
  between operations  13.6 us (6%)
  local copies, waits for them, and re-layouts  8.42 us (4%)
  other arithmetic  4.56 us (2%)
    all_to_all x1, waiting for transfers between devices, local(): lax.all_to_all(packed, ('cuts', 'z'), split_axis=0, concat_axis=0, tiled=...  60.6 us
    all_to_all x1, blocking collectives, local(): lax.all_to_all(both, ('z', 'y'), split_axis=0, concat_axis=0, tiled=True)  46.8 us
    all_gather x1, waiting for transfers between devices, local(): lax.all_gather(payload, ('y', 'core'), axis=0, tiled=True)  30.2 us
    all_gather x1, waiting for transfers between devices, local(): lax.all_gather(w_head.reshape(DH // CUTS, H * DH), ('z', 'cuts'), axis=0,...  13.5 us
    all_to_all x1, starting transfers between devices, local(): lax.all_to_all(packed, ('cuts', 'z'), split_axis=0, concat_axis=0, tiled=...  13.3 us
    pallas_call x1, Pallas kernels, attend(): pl.pallas_call(attend_kernel, out_shape=(piece, piece), in_specs=[smem, s...  13 us
    pallas_call x1, Pallas kernels, pack(): pl.pallas_call(pack_kernel, out_shape=jax.ShapeDtypeStruct((SOURCES, OWN,...  5.23 us
  transfers between devices with their start and end apart: 4, of which 4 were waited for; matrix products, arithmetic and copies ran while one was open for 5% of the time, Pallas kernels for 8%

profile of v5, /device:TPU:8, one launch (start us, length us, event | category | flops | bytes accessed | tf_op | source)
XLA Modules:
  0.0 216.3 jit_solution(15390654833424513293)
XLA Ops:
  6.5 0.0 copy-start
  6.5 0.0 all-gather.3.cloned.1.call-start
  6.5 0.8 reshape.222
  7.3 1.6 pad_maximum_fusion
  8.9 0.0 all-gather.3.cloned.1.call-update
  9.0 5.2 %shard_map.109 = bf16[32,2,128,256]{3,2,1,0:T(8,128)(2,1)} custom-call(s32[1]{0:T(128)} %bitcast.10.self_ref, s32[4,32,64]{2,1,0:T(8,128)} %bitcast.40, s32[4,32,64]{2,1,0:T(8,128)} %bitcast.41, bf16[8,128,2048]{2,1,0:T(8,128)(2,1)} %kv_ref.1), custom_call_target="tpu_custom_call" | custom-call | tf_op jit(solution)/shard_map/pallas_call | solution.py:73
  14.2 13.3 %all-to-all-start = ((bf16[32,2,128,256]{3,2,1,0:T(8,128)(2,1)}), bf16[32,2,128,256]{3,2,1,0:T(8,128)(2,1)}, u32[]{:S(2)}, u32[]{:S(2)}) async-start(bf16[32,2,128,256]{3,2,1,0:T(8,128)(2,1)} %shard_map.109), calls=%async_computation | async-start | bytes 8388608 | tf_op jit(solution)/shard_map/all_to_all | solution.py:259
  27.5 0.0 all-gather.5.cloned.1.call-start
  27.6 30.2 %all-gather.3.cloned.1.call-done = bf16[13312,128]{1,0:T(8,128)(2,1)} async-done(((bf16[832,128]{1,0:T(8,128)(2,1)}), bf16[13312,128]{1,0:T(8,128)(2,1)}) %all-gather.3.cloned.1.call-update) | async-done | bytes 3407888 | tf_op jit(solution)/shard_map/all_gather | solution.py:261
  57.8 1.0 slice.8
  58.8 0.7 reshape.226
  59.5 0.0 all-gather.5.cloned.1.call-update
  59.5 0.7 constant_dynamic-slice_fusion.3
  60.2 0.1 copy.19
  60.3 0.1 eq.36
  60.4 0.2 fusion
  60.7 0.1 copy.20
  60.7 0.1 reshape.220
  60.9 0.1 reshape.218
  61.0 0.0 copy-done
  61.0 1.0 copy.21
  62.0 0.7 fusion.7
  62.7 0.8 gather_fusion.1
  63.5 0.9 gather_fusion
  64.4 0.1 convert_multiply_fusion
  64.5 0.7 mul.52.mask_ref
  65.2 0.7 fusion.6
  65.9 0.7 select_reduce_fusion.pos_ref
  66.6 60.6 %all-to-all-done = bf16[32,2,128,256]{3,2,1,0:T(8,128)(2,1)} async-done(((bf16[32,2,128,256]{3,2,1,0:T(8,128)(2,1)}), bf16[32,2,128,256]{3,2,1,0:T(8,128)(2,1)}, u32[]{:S(2)}, u32[]{:S(2)}) %all-to-all-start) | async-done | bytes 4194336 | tf_op jit(solution)/shard_map/all_to_all | solution.py:259
  127.2 13.0 %shard_map.110 = (bf16[64,96,128]{2,1,0:T(8,128)(2,1)}, bf16[64,96,128]{2,1,0:T(8,128)(2,1)}) custom-call(s32[64]{0:T(128)} %select_reduce_fusion.pos_ref, s32[1]{0:T(128)} %bitcast.3.core_ref, f32[384]{0:T(512)} %mul.52.mask_ref, bf16[16,832,128]{2,1,0:T(8,128)(2,1)} %bitcast.37, bf16[64,128,256]{2,1,0:T(8,128)(2,1)} %bitcast.13.kv_hbm), custom_call_target="tpu_custom_call" | custom-call | flops 805306368 | bytes 10485760 | tf_op jit(solution)/shard_map/pallas_call | solution.py:170
  140.2 1.9 collective-permute-start
  142.1 3.6 %collective-permute-done = bf16[64,96,128]{2,1,0:T(8,128)(2,1)S(1)} collective-permute-done((bf16[64,96,128]{2,1,0:T(8,128)(2,1)}, bf16[64,96,128]{2,1,0:T(8,128)(2,1)S(1)}, u32[]{:S(2)}, u32[]{:S(2)}) %collective-permute-start) | collective-permute-done | bytes 1572896 | tf_op jit(solution)/shard_map/ppermute | solution.py:268
  145.7 1.8 add_convert_fusion
  147.5 0.0 copy-start.2
  147.5 0.0 copy-start.3
  147.6 0.0 copy-start.4
  147.6 13.5 %all-gather.5.cloned.1.call-done.w_ref = bf16[1024,1024]{1,0:T(8,128)(2,1)} async-done(((bf16[32,1024]{1,0:T(8,128)(2,1)}), bf16[1024,1024]{1,0:T(8,128)(2,1)}) %all-gather.5.cloned.1.call-update) | async-done | bytes 2097168 | tf_op jit(solution)/shard_map/all_gather | solution.py:263
  161.1 0.0 copy-start.1
  161.1 46.8 %all_to_all.10.back_ref = bf16[64,96,128]{2,1,0:T(8,128)(2,1)S(1)} all-to-all(bf16[64,96,128]{2,1,0:T(8,128)(2,1)S(1)} %add_convert_fusion), channel_id=1, replica_groups=mesh['cuts'=4,'z'=8,'y'=8,'core'=2] {'z','y'}, dimensions={0} | all-to-all | bytes 3145728 | tf_op jit(solution)/shard_map/all_to_all | solution.py:271
  207.9 0.0 copy-done.2
  207.9 0.0 copy-done.3
  207.9 0.0 copy-done.4
  207.9 0.0 copy-done.1
  208.0 1.5 shard_map.111
  (8 shorter events, 0.1 us)
Async XLA Ops:
  6.5 54.4 %copy-start = (s32[4,64,6,32]{1,3,2,0:T(8,128)S(1)}, s32[4,64,6,32]{1,3,2,0:T(8,128)}, u32[]{:S(2)}) copy-start(s32[4,64,6,32]{1,3,2,0:T(8,128)} %param.21) | copy-start | bytes 589828
  6.5 51.3 %all-gather.3.cloned.1.call-start = ((), (), s32[]{:S(2)}) async-start(), calls=%async_computation.2 | async-start | bytes 3620864 | tf_op jit(solution)/shard_map/all_gather | solution.py:261
  14.2 113.0 %all-to-all-start = ((bf16[32,2,128,256]{3,2,1,0:T(8,128)(2,1)}), bf16[32,2,128,256]{3,2,1,0:T(8,128)(2,1)}, u32[]{:S(2)}, u32[]{:S(2)}) async-start(bf16[32,2,128,256]{3,2,1,0:T(8,128)(2,1)} %shard_map.109), calls=%async_computation | async-start | bytes 8388608 | tf_op jit(solution)/shard_map/all_to_all | solution.py:259
  27.5 133.6 %all-gather.5.cloned.1.call-start = ((), (), s32[]{:S(2)}) async-start(), calls=%async_computation.3 | async-start | bytes 2162688 | tf_op jit(solution)/shard_map/all_gather | solution.py:263
  140.2 5.5 %collective-permute-start = (bf16[64,96,128]{2,1,0:T(8,128)(2,1)}, bf16[64,96,128]{2,1,0:T(8,128)(2,1)S(1)}, u32[]{:S(2)}, u32[]{:S(2)}) collective-permute-start(bf16[64,96,128]{2,1,0:T(8,128)(2,1)} %get-tuple-element.10), channel_id=1, source_target_pairs={{0,1},{1,0},{2,3},{3,2},{4,5},{5,4},{6,7},{7,6},{8,9},{9,8},{10,11... | collective-permute-start | bytes 4718600 | tf_op jit(solution)/shard_map/ppermute | solution.py:268
  147.5 60.4 %copy-start.2 = (bf16[1,16,6,1024]{3,1,2,0:T(8,128)(2,1)S(1)}, bf16[1,16,6,1024]{3,1,2,0:T(8,128)(2,1)}, u32[]{:S(2)}) copy-start(bf16[1,16,6,1024]{3,1,2,0:T(8,128)(2,1)} %param.13) | copy-start | bytes 589828
  147.5 60.4 %copy-start.3 = (bf16[1,16,6,1024]{3,1,2,0:T(8,128)(2,1)S(1)}, bf16[1,16,6,1024]{3,1,2,0:T(8,128)(2,1)}, u32[]{:S(2)}) copy-start(bf16[1,16,6,1024]{3,1,2,0:T(8,128)(2,1)} %param.14) | copy-start | bytes 589828
  147.6 60.4 %copy-start.4 = (f32[1024]{0:T(1024)S(1)}, f32[1024]{0:T(1024)}, u32[]{:S(2)}) copy-start(f32[1024]{0:T(1024)} %param.16) | copy-start | bytes 12292
  161.1 46.8 %copy-start.1 = (bf16[1024,1024]{1,0:T(8,128)(2,1)S(1)}, bf16[1024,1024]{1,0:T(8,128)(2,1)}, u32[]{:S(2)}) copy-start(bf16[1024,1024]{1,0:T(8,128)(2,1)} %all-gather.5.cloned.1.call-done.w_ref) | copy-start | bytes 6291460
Sparse Core Ops, SparseCore 0:
  9.5 48.2 all-gather.2
  61.0 100.0 all-gather.4

commit v6 on v2

--- a/solution.py
+++ b/solution.py
@@ -259,9 +259,14 @@
     arrived = lax.all_to_all(packed, ("cuts", "z"), split_axis=0, concat_axis=0, tiled=True)
     payload = jnp.concatenate([queries.reshape(ROWS_G, DH), w_out.reshape(W_ROWS, DH)], axis=0)
     payload = lax.all_gather(payload, ("y", "core"), axis=0, tiled=True).reshape(GROUPS, PAYLOAD, DH)
-    w_head = payload[:, ROWS_G:].reshape(DH, H * DH)
-    w_all = lax.all_gather(w_head, "z", axis=0, tiled=True)
+    half = lax.dynamic_slice_in_dim(payload[:, ROWS_G:], core * (GROUPS // CORES), GROUPS // CORES)
+    half = lax.all_gather(half.reshape(1, DH // CORES, H * DH), "z", axis=0, tiled=True)
+    swapped = lax.ppermute(half, "core", [(0, 1), (1, 0)])
+    w_all = jnp.stack(
+        [jnp.where(core == 0, half, swapped), jnp.where(core == 0, swapped, half)], axis=1
+    ).reshape(H * DH, H * DH)
     positions, masks = describe(cut, yc, hist_blocks, ranker_list, owner_ids, block_mask)
+    arrived, w_all = lax.optimization_barrier((arrived, w_all))
     keep, send = attend(
         positions, core.reshape(1), masks, payload, arrived.reshape(BLOCKS_HERE, BLK, SLAB)
     )

time: 224 us -> 220 us (0.982)
  blocking collectives: 0 us -> 47.3 us
  waiting for transfers between devices: 144 us -> 102 us
  starting transfers between devices: 29.3 us -> 18.7 us
    all_to_all x0 -> x1, blocking collectives: none -> 47.3 us  [local(): lax.all_to_all(both, ('z', 'y'), split_axis=0, concat_axis=0, tiled=True)]
    all_to_all x1, waiting for transfers between devices: 44.1 us -> 0.01 us  [local(): lax.all_to_all(packed, ('cuts', 'z'), split_axis=0, concat_axis=0, tiled=...]
    all_gather x1, waiting for transfers between devices: 40.7 us -> 31.1 us  [local(): lax.all_gather(payload, ('y', 'core'), axis=0, tiled=True)]
    all_gather x1, waiting for transfers between devices: 57.6 us -> 67.1 us  [local(): lax.all_gather(half.reshape(1, DH // CORES, H * DH), 'z', axis=0, tiled=T...]
    all_to_all x1 -> x0, starting transfers between devices: 7.96 us -> none  [local(): lax.all_to_all(both, ('z', 'y'), split_axis=0, concat_axis=0, tiled=True)]
    ppermute x1, starting transfers between devices: 7.28 us -> 1.92 us  [local(): other = lax.ppermute(send, 'core', [(0, 1), (1, 0)])]
    ppermute x0 -> x1, starting transfers between devices: none -> 2.87 us  [local(): swapped = lax.ppermute(half, 'core', [(0, 1), (1, 0)])]
  transfers between devices with their start and end apart: 5 -> 5, of which waited for: 4 -> 3; matrix products, arithmetic and copies ran while one was open for 6% -> 6% of each run, Pallas kernels for 0% -> 2%
where the time goes in v6:
time: 220 us; the launch traced here: 217 us
  waiting for transfers between devices  102 us (46%)
  blocking collectives  47.3 us (22%)
  Pallas kernels  19.7 us (9%)
  starting transfers between devices  18.7 us (8%)
  between operations  13.6 us (6%)
  local copies, waits for them, and re-layouts  10.7 us (5%)
  other arithmetic  5.62 us (3%)
    all_gather x1, waiting for transfers between devices, local(): lax.all_gather(half.reshape(1, DH // CORES, H * DH), 'z', axis=0, tiled=T...  67.1 us
    all_to_all x1, blocking collectives, local(): lax.all_to_all(both, ('z', 'y'), split_axis=0, concat_axis=0, tiled=True)  47.3 us
    all_gather x1, waiting for transfers between devices, local(): lax.all_gather(payload, ('y', 'core'), axis=0, tiled=True)  31.1 us
    all_to_all x1, starting transfers between devices, local(): lax.all_to_all(packed, ('cuts', 'z'), split_axis=0, concat_axis=0, tiled=...  13.9 us
    pallas_call x1, Pallas kernels, attend(): pl.pallas_call(attend_kernel, out_shape=(piece, piece), in_specs=[smem, s...  13 us
    pallas_call x1, Pallas kernels, pack(): pl.pallas_call(pack_kernel, out_shape=jax.ShapeDtypeStruct((SOURCES, OWN,...  5.19 us
  transfers between devices with their start and end apart: 5, of which 3 were waited for; matrix products, arithmetic and copies ran while one was open for 6% of the time, Pallas kernels for 2%

profile of v6, /device:TPU:1, one launch (start us, length us, event | category | flops | bytes accessed | tf_op | source)
XLA Modules:
  0.0 217.4 jit_solution(12368670906658193773)
XLA Ops:
  6.5 0.0 copy-start
  6.5 0.0 all-gather.3.cloned.1.call-start
  6.5 0.8 reshape.225
  7.3 1.6 pad_maximum_fusion.1
  8.9 0.0 all-gather.3.cloned.1.call-update
  9.0 5.2 %shard_map.109 = bf16[32,2,128,256]{3,2,1,0:T(8,128)(2,1)} custom-call(s32[1]{0:T(128)} %bitcast.10.self_ref, s32[4,32,64]{2,1,0:T(8,128)} %bitcast.46, s32[4,32,64]{2,1,0:T(8,128)} %bitcast.47, bf16[8,128,2048]{2,1,0:T(8,128)(2,1)} %kv_ref.1), custom_call_target="tpu_custom_call" | custom-call | tf_op jit(solution)/shard_map/pallas_call | solution.py:73
  14.2 13.9 %all-to-all-start = ((bf16[32,2,128,256]{3,2,1,0:T(8,128)(2,1)}), bf16[32,2,128,256]{3,2,1,0:T(8,128)(2,1)}, u32[]{:S(2)}, u32[]{:S(2)}) async-start(bf16[32,2,128,256]{3,2,1,0:T(8,128)(2,1)} %shard_map.109), calls=%async_computation | async-start | bytes 8388608 | tf_op jit(solution)/shard_map/all_to_all | solution.py:259
  28.0 0.0 all-gather.5.cloned.1.call-start
  28.1 31.1 %all-gather.3.cloned.1.call-done = bf16[13312,128]{1,0:T(8,128)(2,1)} async-done(((bf16[832,128]{1,0:T(8,128)(2,1)}), bf16[13312,128]{1,0:T(8,128)(2,1)}) %all-gather.3.cloned.1.call-update) | async-done | bytes 3407888 | tf_op jit(solution)/shard_map/all_gather | solution.py:261
  59.2 1.0 slice.8
  60.2 0.7 reshape.228
  60.9 0.0 all-gather.5.cloned.1.call-update
  61.0 0.7 constant_dynamic-slice_fusion.3
  61.7 0.1 copy.26
  61.8 0.1 eq.40
  61.9 0.2 fusion
  62.1 0.1 copy.27
  62.2 0.1 reshape.223
  62.3 0.0 copy-done
  62.3 0.7 constant_dynamic-slice_fusion.2
  63.0 67.1 %all-gather.5.cloned.1.call-done = bf16[8,64,1024]{2,1,0:T(8,128)(2,1)} async-done(((bf16[1,64,1024]{2,1,0:T(8,128)(2,1)}), bf16[8,64,1024]{2,1,0:T(8,128)(2,1)}) %all-gather.5.cloned.1.call-update) | async-done | bytes 1048592 | tf_op jit(solution)/shard_map/all_gather | solution.py:263
  130.2 0.0 copy-start.4
  130.2 2.9 %collective-permute-start = (bf16[8,64,1024]{2,1,0:T(8,128)(2,1)}, bf16[8,64,1024]{2,1,0:T(8,128)(2,1)S(1)}, u32[]{:S(2)}, u32[]{:S(2)}) collective-permute-start(bf16[8,64,1024]{2,1,0:T(8,128)(2,1)} %all-gather.5.cloned.1.call-done), channel_id=1, source_target_pairs={{0,1},{1,0},{2,3},{3,2},{4,5},{5,4},{6,7},{7,6},{8,9},{9,8},{10,11... | collective-permute-start | bytes 3145736 | tf_op jit(solution)/shard_map/ppermute | solution.py:264
  133.0 0.7 fusion.7
  133.7 0.1 reshape.221
  133.8 1.8 copy.28
  135.7 1.5 gather_fusion
  137.2 0.8 gather_fusion.1
  138.0 0.8 convert_multiply_fusion
  138.8 0.7 mul.52.mask_ref
  139.5 0.7 fusion.6
  140.2 0.7 select_reduce_fusion.pos_ref
  140.9 0.0 collective-permute-done
  140.9 0.0 copy-done.4
  140.9 0.1 select_bitcast_fusion.1
  141.1 0.2 pad_maximum_fusion
  141.3 0.2 copy.30
  141.5 0.0 all-to-all-done
  141.5 13.0 %shard_map.110 = (bf16[64,96,128]{2,1,0:T(8,128)(2,1)}, bf16[64,96,128]{2,1,0:T(8,128)(2,1)}) custom-call(s32[64]{0:T(128)} %select_reduce_fusion.pos_ref, s32[1]{0:T(128)} %bitcast.3.core_ref, f32[384]{0:T(512)} %mul.52.mask_ref, bf16[16,832,128]{2,1,0:T(8,128)(2,1)} %bitcast.43, bf16[64,128,256]{2,1,0:T(8,128)(2,1)} %bitcast.16.kv_hbm), custom_call_target="tpu_custom_call" | custom-call | flops 805306368 | bytes 10485760 | tf_op jit(solution)/shard_map/pallas_call | solution.py:170
  154.5 1.9 collective-permute-start.1
  156.4 3.6 %collective-permute-done.1 = bf16[64,96,128]{2,1,0:T(8,128)(2,1)S(1)} collective-permute-done((bf16[64,96,128]{2,1,0:T(8,128)(2,1)}, bf16[64,96,128]{2,1,0:T(8,128)(2,1)S(1)}, u32[]{:S(2)}, u32[]{:S(2)}) %collective-permute-start.1) | collective-permute-done | bytes 1572896 | tf_op jit(solution)/shard_map/ppermute | solution.py:273
  160.0 1.8 add_convert_fusion
  161.8 0.0 copy-start.1
  161.8 0.0 copy-start.2
  161.8 0.0 copy-start.3
  161.8 47.3 %all_to_all.10.back_ref = bf16[64,96,128]{2,1,0:T(8,128)(2,1)S(1)} all-to-all(bf16[64,96,128]{2,1,0:T(8,128)(2,1)S(1)} %add_convert_fusion), channel_id=1, replica_groups=mesh['cuts'=4,'z'=8,'y'=8,'core'=2] {'z','y'}, dimensions={0} | all-to-all | bytes 3145728 | tf_op jit(solution)/shard_map/all_to_all | solution.py:275
  209.1 0.0 copy-done.1
  209.1 0.0 copy-done.2
  209.1 0.0 copy-done.3
  209.1 1.5 shard_map.111
  (7 shorter events, 0.1 us)
Async XLA Ops:
  6.5 55.8 %copy-start = (s32[4,64,6,32]{1,3,2,0:T(8,128)S(1)}, s32[4,64,6,32]{1,3,2,0:T(8,128)}, u32[]{:S(2)}) copy-start(s32[4,64,6,32]{1,3,2,0:T(8,128)} %param.21) | copy-start | bytes 589828
  6.5 52.7 %all-gather.3.cloned.1.call-start = ((), (), s32[]{:S(2)}) async-start(), calls=%async_computation.2 | async-start | bytes 3620864 | tf_op jit(solution)/shard_map/all_gather | solution.py:261
  14.2 127.3 %all-to-all-start = ((bf16[32,2,128,256]{3,2,1,0:T(8,128)(2,1)}), bf16[32,2,128,256]{3,2,1,0:T(8,128)(2,1)}, u32[]{:S(2)}, u32[]{:S(2)}) async-start(bf16[32,2,128,256]{3,2,1,0:T(8,128)(2,1)} %shard_map.109), calls=%async_computation | async-start | bytes 8388608 | tf_op jit(solution)/shard_map/all_to_all | solution.py:259
  28.0 102.1 %all-gather.5.cloned.1.call-start = ((), (), s32[]{:S(2)}) async-start(), calls=%async_computation.3 | async-start | bytes 1179648 | tf_op jit(solution)/shard_map/all_gather | solution.py:263
  130.2 10.8 %copy-start.4 = (bf16[8,64,1024]{2,1,0:T(8,128)(2,1)S(1)}, bf16[8,64,1024]{2,1,0:T(8,128)(2,1)}, u32[]{:S(2)}) copy-start(bf16[8,64,1024]{2,1,0:T(8,128)(2,1)} %all-gather.5.cloned.1.call-done) | copy-start | bytes 3145732
  130.2 10.8 %collective-permute-start = (bf16[8,64,1024]{2,1,0:T(8,128)(2,1)}, bf16[8,64,1024]{2,1,0:T(8,128)(2,1)S(1)}, u32[]{:S(2)}, u32[]{:S(2)}) collective-permute-start(bf16[8,64,1024]{2,1,0:T(8,128)(2,1)} %all-gather.5.cloned.1.call-done), channel_id=1, source_target_pairs={{0,1},{1,0},{2,3},{3,2},{4,5},{5,4},{6,7},{7,6},{8,9},{9,8},{10,11... | collective-permute-start | bytes 3145736 | tf_op jit(solution)/shard_map/ppermute | solution.py:264
  154.5 5.5 %collective-permute-start.1 = (bf16[64,96,128]{2,1,0:T(8,128)(2,1)}, bf16[64,96,128]{2,1,0:T(8,128)(2,1)S(1)}, u32[]{:S(2)}, u32[]{:S(2)}) collective-permute-start(bf16[64,96,128]{2,1,0:T(8,128)(2,1)} %get-tuple-element.11), channel_id=1, source_target_pairs={{0,1},{1,0},{2,3},{3,2},{4,5},{5,4},{6,7},{7,6},{8,9},{9,8},{10,11... | collective-permute-start | bytes 4718600 | tf_op jit(solution)/shard_map/ppermute | solution.py:273
  161.8 47.3 %copy-start.1 = (bf16[1,16,6,1024]{3,1,2,0:T(8,128)(2,1)S(1)}, bf16[1,16,6,1024]{3,1,2,0:T(8,128)(2,1)}, u32[]{:S(2)}) copy-start(bf16[1,16,6,1024]{3,1,2,0:T(8,128)(2,1)} %param.13) | copy-start | bytes 589828
  161.8 47.3 %copy-start.2 = (bf16[1,16,6,1024]{3,1,2,0:T(8,128)(2,1)S(1)}, bf16[1,16,6,1024]{3,1,2,0:T(8,128)(2,1)}, u32[]{:S(2)}) copy-start(bf16[1,16,6,1024]{3,1,2,0:T(8,128)(2,1)} %param.14) | copy-start | bytes 589828
  161.8 47.3 %copy-start.3 = (f32[1024]{0:T(1024)S(1)}, f32[1024]{0:T(1024)}, u32[]{:S(2)}) copy-start(f32[1024]{0:T(1024)} %param.16) | copy-start | bytes 12292
Sparse Core Ops, SparseCore 0:
  9.5 49.7 all-gather.2
  61.3 68.7 all-gather.4
